TPU v7x, 32 devices: a whole 2x2x4 slice. The times are simulated.
32 devices in a mesh: group: 8 (over y, x, core), mp: 4 (over z).
Axes of the slice: x: 2, y: 2, z: 4, core: 2. Of those that a mesh axis runs over, the one named last changes fastest.
Arguments:
- hidden_in: bfloat16 [4096, 1024], P('group'), may hold values from -8 to 8
- request_ids: int32 [4096], P('group'), may hold values from 63 to 4095, as said below
- w_qkv: float32 [1024, 3072], P(('group', 'mp')), may hold values from -1 to 1
- w_out: float32 [1024, 1024], P(('group', 'mp')), may hold values from -0.1875 to 0.1875
- w_up: float32 [1024, 4096], P(('group', 'mp')), may hold values from -0.1875 to 0.1875
- w_down: float32 [1024, 4096], P(('group', 'mp')), may hold values from -0.09375 to 0.09375
- ln1_gain: float32 [1024], replicated, may hold values from 0.25 to 1.75
- ln1_shift: float32 [1024], replicated, may hold values from -3 to 3
- ln2_gain: float32 [1024], replicated, may hold values from 0.25 to 1.75
- ln2_shift: float32 [1024], replicated, may hold values from -3 to 3
Outputs:
- hidden_out: bfloat16 [4096, 1024], P(('group', 'mp'))
- keys_cache: bfloat16 [4096, 1024], P('group', 'mp')
- values_cache: bfloat16 [4096, 1024], P('group', 'mp')
Inputs may be any that keep to these rules, and one draw needn't show every extreme that they name: `request_ids`: each slot holds the index of the last slot of its request. In groups 2i and 2i+1 (of 512 slots each) one request of exactly 512 slots ends the first group and begins the second, at least 64 of its slots in each; every other request lies within one aligned block of 64 slots, one or two requests a block, and some blocks hold one request of exactly 64 slots.
All inputs are finite; a program needn't handle non-finite values.
Results may differ from a plain program's by a relative error of at most 0.011.
Values may be sent and summed in bfloat16 or wider, within the bound.
A program may use at most 64 MiB of HBM per device.

v0:
```python
import jax
import jax.numpy as jnp
from jax import lax
from jax.sharding import PartitionSpec as P

HD = 64
SHORT = 64


def swapped(value, axis, distance):
    return lax.ppermute(value, axis, [(i, i ^ 1 << distance) for i in range(lax.axis_size(axis))])


def layer_norm(values_in, norm_gain, norm_shift):
    center = values_in - jnp.mean(values_in, axis=-1, keepdims=True)
    spread = jnp.mean(center * center, axis=-1, keepdims=True)
    return center * lax.rsqrt(spread + 1e-05) * norm_gain + norm_shift


def body(
    hidden_in, request_ids, w_qkv, w_out, w_up, w_down, ln1_gain, ln1_shift, ln2_gain, ln2_shift
):
    groups = lax.axis_size("group")
    shards = lax.axis_size("mp")
    model_width = hidden_in.shape[1]
    local_width = model_width // shards
    local_hidden = w_up.shape[1] // shards
    tok_rows = hidden_in.shape[0]
    part_rows = w_qkv.shape[0]
    pieces = (
        w_qkv.astype(jnp.bfloat16).reshape(part_rows, 3, shards, local_width),
        w_out.astype(jnp.bfloat16).reshape(part_rows, 1, shards, local_width),
        w_up.astype(jnp.bfloat16).reshape(part_rows, 1, shards, local_hidden),
        w_down.astype(jnp.bfloat16).reshape(part_rows, 1, shards, local_hidden),
    )
    gathered = (
        lax.all_gather(pieces[0], "group", axis=0, tiled=True),
        lax.all_gather(pieces[1], "group", axis=0, tiled=True),
        lax.all_gather(pieces[2], "group", axis=0, tiled=True),
        lax.all_gather(pieces[3], "group", axis=0, tiled=True),
    )
    exchanged = (
        lax.all_to_all(gathered[0], "mp", split_axis=2, concat_axis=0, tiled=True),
        lax.all_to_all(gathered[1], "mp", split_axis=2, concat_axis=0, tiled=True),
        lax.all_to_all(gathered[2], "mp", split_axis=2, concat_axis=0, tiled=True),
        lax.all_to_all(gathered[3], "mp", split_axis=2, concat_axis=0, tiled=True),
    )
    served = tuple(
        (
            jnp.transpose(
                weight_piece.reshape(shards, groups, part_rows, -1), (1, 0, 2, 3)
            ).reshape(model_width, -1)
            for weight_piece in exchanged
        )
    )
    qkv_local, out_local, up_local, down_local = served
    projected = jnp.dot(hidden_in, qkv_local, preferred_element_type=jnp.float32)
    queries = projected[:, :local_width].astype(jnp.bfloat16)
    key_rows = projected[:, local_width : 2 * local_width].astype(jnp.bfloat16)
    value_rows = projected[:, 2 * local_width :].astype(jnp.bfloat16)
    partner_keys, partner_values = swapped((key_rows, value_rows), "group", 0)
    group_index = lax.axis_index("group")
    parity = group_index % 2
    long_id = jnp.where(parity == 0, request_ids[-1], request_ids[0])
    own_long = request_ids == long_id
    local_heads = local_width // HD
    score_scale = HD ** (-0.5)
    block_total = tok_rows // SHORT
    short_q = queries.reshape(block_total, SHORT, local_heads, HD)
    short_k = key_rows.reshape(block_total, SHORT, local_heads, HD)
    short_v = value_rows.reshape(block_total, SHORT, local_heads, HD)
    short_ids = request_ids.reshape(block_total, SHORT)
    short_scores = (
        jnp.einsum("bqhd,bkhd->bhqk", short_q, short_k, preferred_element_type=jnp.float32)
        * score_scale
    )
    short_mask = short_ids[:, :, None] == short_ids[:, None, :]
    short_scores = jnp.where(short_mask[:, None], short_scores, -1e30)
    short_peak = jnp.max(short_scores, axis=-1, keepdims=True)
    short_weights = jnp.exp(short_scores - short_peak).astype(jnp.bfloat16)
    short_totals = jnp.sum(short_weights.astype(jnp.float32), axis=-1)
    short_mixed = jnp.einsum(
        "bhqk,bkhd->bqhd", short_weights, short_v, preferred_element_type=jnp.float32
    )
    short_out = (
        (short_mixed / jnp.transpose(short_totals, (0, 2, 1))[:, :, :, None])
        .astype(jnp.bfloat16)
        .reshape(tok_rows, local_width)
    )
    first_keys = jnp.where(parity == 0, key_rows, partner_keys)
    second_keys = jnp.where(parity == 0, partner_keys, key_rows)
    first_values = jnp.where(parity == 0, value_rows, partner_values)
    second_values = jnp.where(parity == 0, partner_values, value_rows)
    pair_base = (group_index - parity) * tok_rows
    span_start = long_id - tok_rows + 1 - pair_base
    long_keys = lax.dynamic_slice_in_dim(
        jnp.concatenate([first_keys, second_keys], 0), span_start, tok_rows, 0
    ).reshape(tok_rows, local_heads, HD)
    long_values = lax.dynamic_slice_in_dim(
        jnp.concatenate([first_values, second_values], 0), span_start, tok_rows, 0
    ).reshape(tok_rows, local_heads, HD)
    query_rows = min(512, tok_rows)
    query_blocks = tok_rows // query_rows

    def long_attend(block_queries):
        heads_view = block_queries.reshape(query_rows, local_heads, HD)
        scores = (
            jnp.einsum("qhd,khd->hqk", heads_view, long_keys, preferred_element_type=jnp.float32)
            * score_scale
        )
        row_peak = jnp.max(scores, axis=-1, keepdims=True)
        weights = jnp.exp(scores - row_peak).astype(jnp.bfloat16)
        totals = jnp.sum(weights.astype(jnp.float32), axis=-1)
        mixed_heads = jnp.einsum(
            "hqk,khd->qhd", weights, long_values, preferred_element_type=jnp.float32
        )
        return (
            (mixed_heads / jnp.transpose(totals)[:, :, None])
            .astype(jnp.bfloat16)
            .reshape(query_rows, local_width)
        )

    def skipped(block_queries):
        return jnp.zeros((query_rows, local_width), jnp.bfloat16)

    def long_block(query_block):
        block_queries, block_long = query_block
        return lax.cond(jnp.any(block_long), long_attend, skipped, block_queries)

    long_out = lax.map(
        long_block,
        (
            queries.reshape(query_blocks, query_rows, local_width),
            own_long.reshape(query_blocks, query_rows),
        ),
    ).reshape(tok_rows, local_width)
    attended = jnp.where(own_long[:, None], long_out, short_out)
    share_rows = tok_rows // shards
    row_start = lax.axis_index("mp") * share_rows

    def combine(term_fn, residual, norm_gain, norm_shift):
        summed = lax.psum(term_fn(0, tok_rows), "mp")
        whole_rows = layer_norm(
            residual.astype(jnp.float32) + summed, norm_gain, norm_shift
        ).astype(jnp.bfloat16)
        normed = lax.dynamic_slice_in_dim(whole_rows, row_start, share_rows, 0)
        return (normed, whole_rows)

    def attn_term(row_begin, row_count):
        return lax.dot_general(
            attended, out_local, (((1,), (1,)), ((), ())), preferred_element_type=jnp.float32
        )

    attn_share, attn_normed = combine(attn_term, hidden_in, ln1_gain, ln1_shift)
    activated = jax.nn.gelu(
        jnp.dot(attn_normed, up_local, preferred_element_type=jnp.float32), approximate=False
    ).astype(jnp.bfloat16)

    def feed_term(row_begin, row_count):
        return lax.dot_general(
            activated, down_local, (((1,), (1,)), ((), ())), preferred_element_type=jnp.float32
        )

    final_share, unused = combine(feed_term, attn_normed, ln2_gain, ln2_shift)
    return (final_share, key_rows, value_rows)


def solution(mesh):
    in_specs = (
        P("group", None),
        P("group"),
        P(("group", "mp"), None),
        P(("group", "mp"), None),
        P(("group", "mp"), None),
        P(("group", "mp"), None),
        P(),
        P(),
        P(),
        P(),
    )
    out_specs = (P(("group", "mp"), None), P("group", "mp"), P("group", "mp"))
    return jax.shard_map(body, mesh=mesh, in_specs=in_specs, out_specs=out_specs, check_vma=False)
```

profile of v0, /device:TPU:21, one launch (start us, length us, event | category | flops | bytes accessed | tf_op | source)
XLA Modules:
  0.0 370.8 jit_solution(20624162096457766)
XLA Ops:
  7.2 1.0 convert_element_type.66
  9.2 1.1 convert_element_type.73
  10.2 0.9 reshape.149
  11.2 10.4 %all_gather.13 = bf16[256,1,4,256]{3,2,1,0:T(4,128)(2,1)S(1)} all-gather(bf16[32,1,4,256]{3,2,1,0:T(4,128)(2,1)S(1)} %bitcast.92), channel_id=1, replica_groups=mesh['group'=8,'mp'=4] {'group'}, dimensions={0}, use_global_device_ids=true | all-gather | bytes 589824 | tf_op jit(solution)/shard_map/all_gather | solution.py:38
  21.6 0.9 copy.117
  22.5 4.6 %all-to-all-start.1 = ((bf16[256,1,4,256]{3,0,1,2:T(8,128)(2,1)}), bf16[256,1,4,256]{3,0,1,2:T(8,128)(2,1)S(1)}, u32[]{:S(2)}, u32[]{:S(2)}) async-start(bf16[256,1,4,256]{3,0,1,2:T(8,128)(2,1)} %copy.117), calls=%async_computation.1 | async-start | bytes 1048576 | tf_op jit(solution)/shard_map/all_to_all | solution.py:44
  27.1 10.5 %all-gather.4.cloned.1.call-done = bf16[256,3,4,256]{3,2,1,0:T(4,128)(2,1)} async-done(((bf16[32,3,4,256]{3,2,1,0:T(4,128)(2,1)}), bf16[256,3,4,256]{3,2,1,0:T(4,128)(2,1)}) %all-gather.4.cloned.1.call-update) | async-done | bytes 1572880 | tf_op jit(solution)/shard_map/all_gather | solution.py:37
  37.6 2.8 copy.105
  40.4 4.7 %all-to-all-start = ((bf16[256,3,4,256]{3,0,1,2:T(8,128)(2,1)}), bf16[256,3,4,256]{3,0,1,2:T(8,128)(2,1)S(1)}, u32[]{:S(2)}, u32[]{:S(2)}) async-start(bf16[256,3,4,256]{3,0,1,2:T(8,128)(2,1)} %copy.105), calls=%async_computation | async-start | bytes 3145728 | tf_op jit(solution)/shard_map/all_to_all | solution.py:43
  45.1 0.9 reshape.152
  46.0 21.9 %all-gather.6.cloned.1.call-done = bf16[256,1,4,1024]{3,2,1,0:T(4,128)(2,1)} async-done(((bf16[32,1,4,1024]{3,2,1,0:T(4,128)(2,1)}), bf16[256,1,4,1024]{3,2,1,0:T(4,128)(2,1)}) %all-gather.6.cloned.1.call-update) | async-done | bytes 2097168 | tf_op jit(solution)/shard_map/all_gather | solution.py:39
  67.9 3.6 copy.120
  71.5 7.0 %all-to-all-done = bf16[256,3,4,256]{3,0,1,2:T(8,128)(2,1)S(1)} async-done(((bf16[256,3,4,256]{3,0,1,2:T(8,128)(2,1)}), bf16[256,3,4,256]{3,0,1,2:T(8,128)(2,1)S(1)}, u32[]{:S(2)}, u32[]{:S(2)}) %all-to-all-start) | async-done | bytes 1572896 | tf_op jit(solution)/shard_map/all_to_all | solution.py:43
  78.5 7.4 %all-to-all-start.2 = ((bf16[256,1,4,1024]{3,0,1,2:T(8,128)(2,1)}), bf16[256,1,4,1024]{3,0,1,2:T(8,128)(2,1)}, u32[]{:S(2)}, u32[]{:S(2)}) async-start(bf16[256,1,4,1024]{3,0,1,2:T(8,128)(2,1)} %copy.120), calls=%async_computation.2 | async-start | bytes 4194304 | tf_op jit(solution)/shard_map/all_to_all | solution.py:45
  90.2 8.2 %all-gather.8.cloned.1.call-done = bf16[256,1,4,1024]{3,2,1,0:T(4,128)(2,1)} async-done(((bf16[32,1,4,1024]{3,2,1,0:T(4,128)(2,1)}), bf16[256,1,4,1024]{3,2,1,0:T(4,128)(2,1)}) %all-gather.8.cloned.1.call-update) | async-done | bytes 2097168 | tf_op jit(solution)/shard_map/all_gather | solution.py:40
  98.3 3.7 copy.123
  102.0 1.4 copy.106
  103.4 2.9 reshape.140
  106.3 1.6 copy.107
  108.0 1.0 convolution_convert_fusion
  108.9 0.8 fusion.97
  110.1 1.2 reshape.144
  112.3 1.0 copy-done.13
  113.5 2.0 reshape.142
  115.6 15.0 %all-to-all-done.2 = bf16[256,1,4,1024]{3,0,1,2:T(8,128)(2,1)} async-done(((bf16[256,1,4,1024]{3,0,1,2:T(8,128)(2,1)}), bf16[256,1,4,1024]{3,0,1,2:T(8,128)(2,1)}, u32[]{:S(2)}, u32[]{:S(2)}) %all-to-all-start.2) | async-done | bytes 2097184 | tf_op jit(solution)/shard_map/all_to_all | solution.py:45
  130.6 6.7 %all-to-all-start.3 = ((bf16[256,1,4,1024]{3,0,1,2:T(8,128)(2,1)}), bf16[256,1,4,1024]{3,0,1,2:T(8,128)(2,1)S(1)}, u32[]{:S(2)}, u32[]{:S(2)}) async-start(bf16[256,1,4,1024]{3,0,1,2:T(8,128)(2,1)} %copy.123), calls=%async_computation.3 | async-start | bytes 4194304 | tf_op jit(solution)/shard_map/all_to_all | solution.py:46
  137.3 3.0 fusion.20
  140.3 2.2 copy.115
  142.5 2.1 reshape.145
  144.6 1.1 broadcast_select_fusion.1
  145.6 1.1 broadcast_select_fusion.3
  146.7 1.0 pad_maximum_fusion
  147.8 10.7 %conditional.1 = (bf16[512,256]{0,1:T(8,128)(2,1)S(1)}) conditional(s32[]{:T(128)} %convert_element_type.65, () %tuple.28, (s32[]{:T(128)}, s32[]{:T(128)}, s32[]{:T(128)}, bf16[1024,256]{1,0:T(8,128)(2,1)}, bf16[512,256]{1,0:T(8,128)(2,1)S(1)}, /*index=5*/bf16[1024,256]{1,0:T(8,128)(2,1)}) %tuple.29), branch_computations={%region_1.2_spmd, %region_2.5_spmd} | conditional | flops 279179264 | bytes 18391162 | solution.py:128
  147.8 2.1 copy.108
  149.8 2.1 copy.110
  151.9 2.1 constant_dynamic-slice_fusion
  154.0 0.9 copy.109
  154.9 1.8 bitcast_reduce_fusion
  157.7 0.8 fusion.3
  158.5 3.0 fusion.61
  161.5 3.2 copy.121
  164.8 39.7 %all-to-all-done.3 = bf16[256,1,4,1024]{3,0,1,2:T(8,128)(2,1)S(1)} async-done(((bf16[256,1,4,1024]{3,0,1,2:T(8,128)(2,1)}), bf16[256,1,4,1024]{3,0,1,2:T(8,128)(2,1)S(1)}, u32[]{:S(2)}, u32[]{:S(2)}) %all-to-all-start.3) | async-done | bytes 2097184 | tf_op jit(solution)/shard_map/all_to_all | solution.py:46
  204.4 1.6 copy.124
  206.0 55.8 %all-reduce.3.cloned.1.call-done = f32[512,1024]{1,0:T(8,128)} async-done(((f32[512,1024]{1,0:T(8,128)}), f32[512,1024]{1,0:T(8,128)}) %all-reduce.3.cloned.1.call-update) | async-done | bytes 2097168 | tf_op jit(solution)/shard_map/psum | solution.py:142
  261.8 2.0 fusion.53
  265.1 9.8 %fusion.21 = f32[512,1024]{1,0:T(8,128)} fusion(bf16[1024,1024]{1,0:T(8,128)(2,1)} %bitcast.83, bf16[512,1024]{1,0:T(8,128)(2,1)S(1)} %add_convert_fusion, bf16[1024,1024]{1,0:T(8,128)(2,1)} %bitcast.82), kind=kOutput, calls=%fused_computation.43 | convolution fusion | flops 2181562368 | bytes 7340032 | tf_op jit(solution)/shard_map/dot_general | solution.py:160
  274.9 85.6 %all-reduce.5.cloned.1.call-done = f32[512,1024]{1,0:T(8,128)} async-done(((f32[512,1024]{1,0:T(8,128)}), f32[512,1024]{1,0:T(8,128)}) %all-reduce.5.cloned.1.call-update) | async-done | bytes 2097168 | tf_op jit(solution)/shard_map/psum | solution.py:142
  360.5 2.0 fusion.17
  (64 shorter events, 8.9 us)
Async XLA Ops:
  7.2 4.0 %copy-start.7 = (f32[32,1024]{1,0:T(8,128)S(1)}, f32[32,1024]{1,0:T(8,128)}, u32[]{:S(2)}) copy-start(f32[32,1024]{1,0:T(8,128)} %param.15) | copy-start | bytes 393220
  7.2 30.4 %all-gather.4.cloned.1.call-start = ((), (), s32[]{:S(2)}) async-start(), calls=%async_computation.4 | async-start | bytes 1769472 | tf_op jit(solution)/shard_map/all_gather | solution.py:37
  9.1 58.8 %all-gather.6.cloned.1.call-start = ((), (), s32[]{:S(2)}) async-start(), calls=%async_computation.6 | async-start | bytes 2359296 | tf_op jit(solution)/shard_map/all_gather | solution.py:39
  22.5 17.9 %all-to-all-start.1 = ((bf16[256,1,4,256]{3,0,1,2:T(8,128)(2,1)}), bf16[256,1,4,256]{3,0,1,2:T(8,128)(2,1)S(1)}, u32[]{:S(2)}, u32[]{:S(2)}) async-start(bf16[256,1,4,256]{3,0,1,2:T(8,128)(2,1)} %copy.117), calls=%async_computation.1 | async-start | bytes 1048576 | tf_op jit(solution)/shard_map/all_to_all | solution.py:44
  40.4 4.7 %copy-start.5 = (f32[32,4096]{1,0:T(8,128)S(1)}, f32[32,4096]{1,0:T(8,128)}, u32[]{:S(2)}) copy-start(f32[32,4096]{1,0:T(8,128)} %param.17) | copy-start | bytes 1572868
  40.4 38.2 %all-to-all-start = ((bf16[256,3,4,256]{3,0,1,2:T(8,128)(2,1)}), bf16[256,3,4,256]{3,0,1,2:T(8,128)(2,1)S(1)}, u32[]{:S(2)}, u32[]{:S(2)}) async-start(bf16[256,3,4,256]{3,0,1,2:T(8,128)(2,1)} %copy.105), calls=%async_computation | async-start | bytes 3145728 | tf_op jit(solution)/shard_map/all_to_all | solution.py:43
  45.1 53.3 %all-gather.8.cloned.1.call-start = ((), (), s32[]{:S(2)}) async-start(), calls=%async_computation.7 | async-start | bytes 2359296 | tf_op jit(solution)/shard_map/all_gather | solution.py:40
  71.5 14.4 %copy-start.8 = (s32[512]{0:T(512)S(1)}, s32[512]{0:T(512)}, u32[]{:S(2)}) copy-start(s32[512]{0:T(512)} %param.13) | copy-start | bytes 6148
  78.5 7.4 %copy-start.3 = (bf16[256,3,4,256]{3,0,1,2:T(8,128)(2,1)}, bf16[256,3,4,256]{3,0,1,2:T(8,128)(2,1)S(1)}, u32[]{:S(2)}) copy-start(bf16[256,3,4,256]{3,0,1,2:T(8,128)(2,1)S(1)} %all-to-all-done) | copy-start | bytes 4718596
  78.5 52.1 %all-to-all-start.2 = ((bf16[256,1,4,1024]{3,0,1,2:T(8,128)(2,1)}), bf16[256,1,4,1024]{3,0,1,2:T(8,128)(2,1)}, u32[]{:S(2)}, u32[]{:S(2)}) async-start(bf16[256,1,4,1024]{3,0,1,2:T(8,128)(2,1)} %copy.120), calls=%async_computation.2 | async-start | bytes 4194304 | tf_op jit(solution)/shard_map/all_to_all | solution.py:45
  98.3 3.7 copy-start.4
  106.3 1.7 copy-start.1
  109.8 35.9 %collective-permute-start = (bf16[512,256]{1,0:T(8,128)(2,1)}, bf16[512,256]{1,0:T(8,128)(2,1)}, u32[]{:S(2)}, u32[]{:S(2)}) collective-permute-start(bf16[512,256]{1,0:T(8,128)(2,1)} %get-tuple-element.165), channel_id=1, source_target_pairs={{0,4},{4,0},{8,12},{12,8},{16,20},{20,16},{24,28},{28,24},{1,5},{5... | collective-permute-start | bytes 786440 | tf_op jit(solution)/shard_map/ppermute | solution.py:11
  111.3 33.3 %collective-permute-start.1 = (bf16[512,256]{1,0:T(8,128)(2,1)}, bf16[512,256]{1,0:T(8,128)(2,1)}, u32[]{:S(2)}, u32[]{:S(2)}) collective-permute-start(bf16[512,256]{1,0:T(8,128)(2,1)} %get-tuple-element.163), channel_id=1, source_target_pairs={{0,4},{4,0},{8,12},{12,8},{16,20},{20,16},{24,28},{28,24},{1,5},{5... | collective-permute-start | bytes 786440 | tf_op jit(solution)/shard_map/ppermute | solution.py:11
  112.3 1.0 copy-start.13
  130.6 73.8 %all-to-all-start.3 = ((bf16[256,1,4,1024]{3,0,1,2:T(8,128)(2,1)}), bf16[256,1,4,1024]{3,0,1,2:T(8,128)(2,1)S(1)}, u32[]{:S(2)}, u32[]{:S(2)}) async-start(bf16[256,1,4,1024]{3,0,1,2:T(8,128)(2,1)} %copy.123), calls=%async_computation.3 | async-start | bytes 4194304 | tf_op jit(solution)/shard_map/all_to_all | solution.py:46
  137.3 124.5 %all-reduce.3.cloned.1.call-start = ((), (), s32[]{:S(2)}) async-start(), calls=%async_computation.5 | async-start | bytes 4194304 | tf_op jit(solution)/shard_map/psum | solution.py:142
  156.7 1.0 copy-start.6
  161.5 199.0 %all-reduce.5.cloned.1.call-start = ((), (), s32[]{:S(2)}) async-start(), calls=%async_computation.8 | async-start | bytes 4194304 | tf_op jit(solution)/shard_map/psum | solution.py:142
  261.8 2.2 copy-start
  263.8 0.7 copy-start.9
  263.8 0.7 copy-start.10
  360.5 2.2 copy-start.2
  362.7 0.7 copy-start.11
  362.7 0.7 copy-start.12
Sparse Core Ops, SparseCore 0:
  10.5 27.0 all-gather.3
  40.0 27.8 all-gather.5
  70.4 27.8 all-gather.7
  161.6 100.1 all-reduce.2
  275.0 85.4 all-reduce.4
where the time goes:
time: 375 us; the launch traced here: 371 us
  waiting for transfers between devices  244 us (65%)
  local copies, waits for them, and re-layouts  43.4 us (12%)
  starting transfers between devices  24.1 us (6%)
  matrix products  19.8 us (5%)
  between operations  15.9 us (4%)
  other arithmetic  13.4 us (4%)
  blocking collectives  10.4 us (3%)
    psum x2, waiting for transfers between devices, combine(): summed = lax.psum(term_fn(0, tok_rows), 'mp')  141 us
    all_to_all x1, waiting for transfers between devices, body(): lax.all_to_all(gathered[3], 'mp', split_axis=2, concat_axis=0, tiled=True)  39.7 us
    all_gather x1, waiting for transfers between devices, body(): lax.all_gather(pieces[2], 'group', axis=0, tiled=True)  21.9 us
    all_to_all x1, waiting for transfers between devices, body(): lax.all_to_all(gathered[2], 'mp', split_axis=2, concat_axis=0, tiled=True)  15 us
    all_gather x1, waiting for transfers between devices, body(): lax.all_gather(pieces[0], 'group', axis=0, tiled=True)  10.5 us
    all_gather x1, blocking collectives, body(): lax.all_gather(pieces[1], 'group', axis=0, tiled=True)  10.4 us
    dot_general x1, matrix products, feed_term(): lax.dot_general(activated, down_local, (((1,), (1,)), ((), ())), preferre...  9.77 us
    all_gather x1, waiting for transfers between devices, body(): lax.all_gather(pieces[3], 'group', axis=0, tiled=True)  8.17 us
  transfers between devices with their start and end apart: 11, of which 8 were waited for; matrix products, arithmetic and copies ran while one was open for 15% of the time, Pallas kernels for 0%

commit v1 on v0

--- a/solution.py
+++ b/solution.py
@@ -1,6 +1,10 @@
+import functools
+
 import jax
 import jax.numpy as jnp
 from jax import lax
+from jax.experimental import pallas as pl
+from jax.experimental.pallas import tpu as pltpu
 from jax.sharding import PartitionSpec as P
 
 HD = 64
@@ -17,7 +21,7 @@
     return center * lax.rsqrt(spread + 1e-05) * norm_gain + norm_shift
 
 
-def body(
+def plain_body(
     hidden_in, request_ids, w_qkv, w_out, w_up, w_down, ln1_gain, ln1_shift, ln2_gain, ln2_shift
 ):
     groups = lax.axis_size("group")
@@ -165,6 +169,330 @@
     return (final_share, key_rows, value_rows)
 
 
+MESH = pl.DeviceIdType.MESH
+Q, O, U, W = range(4)
+
+
+def layer_kernel(
+    shards, hid, id_col, id_row, w_qkv, w_out, w_up, w_down, gain1, shift1, gain2, shift2,
+    out, k_out, v_out,
+    stage_q, stage_o, stage_u, stage_d, full_q, full_o, full_u, full_d,
+    bias, queries, keys, vals, att, sums, normed, act, rs_send, rs_recv,
+    z_send, z_recv, p_send, p_recv, kv_send, kv_recv, a_send, a_recv, r_send, r_recv,
+):
+    g = lax.axis_index("group")
+    m = lax.axis_index("mp")
+    core = lax.rem(g, 2)
+    sib = g + 1 - 2 * core
+    gx = g + 2 - 4 * lax.rem(g // 2, 2)
+    gy = g + 4 - 8 * (g // 4)
+    gd = gx + gy - g
+    rows = hid.shape[0]
+    width = hid.shape[1]
+    part = w_qkv.shape[0]
+    lw = queries.shape[1]
+    lh = act.shape[1]
+    pairs = lw // 128
+    share = rows // shards
+    f32, b16 = jnp.float32, jnp.bfloat16
+    fulls = (full_q, full_o, full_u, full_d)
+    stages = (stage_q, stage_o, stage_u, stage_d)
+    peers = [lax.rem(m + k, shards) for k in range(1, shards)]
+    mine = g * shards + m
+
+    def z_copy(kind, k):
+        chunk = stages[kind].at[0] if kind == O else stages[kind].at[peers[k]]
+        return pltpu.make_async_remote_copy(
+            src_ref=chunk, dst_ref=fulls[kind].at[mine],
+            send_sem=z_send.at[kind, k], recv_sem=z_recv.at[kind, k],
+            device_id=(g, peers[k]), device_id_type=MESH)
+
+    fwd_to = gy * (1 - core) + gx * core
+    fwd_block = gx * (1 - core) + gy * core
+    hops = ((g, gx), (g, gy), (fwd_block, fwd_to), (g, sib), (gx, sib), (gy, sib), (gd, sib))
+
+    def p_copy(kind, step):
+        block, target = hops[step]
+        place = fulls[kind].at[pl.ds(block * shards, shards)]
+        return pltpu.make_async_remote_copy(
+            src_ref=place, dst_ref=place,
+            send_sem=p_send.at[kind, step], recv_sem=p_recv.at[kind, step],
+            device_id=(target, m), device_id_type=MESH)
+
+    def first_hop(kind):
+        for k in range(shards - 1):
+            z_copy(kind, k).wait_recv()
+        for step in (0, 1, 3):
+            p_copy(kind, step).start()
+
+    def second_hop(kind):
+        p_copy(kind, 0).wait_recv()
+        p_copy(kind, 1).wait_recv()
+        for step in (2, 4, 5):
+            p_copy(kind, step).start()
+
+    def third_hop(kind):
+        p_copy(kind, 2).wait_recv()
+        p_copy(kind, 6).start()
+
+    def finish(kind):
+        for step in (3, 4, 5, 6):
+            p_copy(kind, step).wait_recv()
+
+    def kv_copy(buf, i):
+        return pltpu.make_async_remote_copy(
+            src_ref=buf.at[0], dst_ref=buf.at[1],
+            send_sem=kv_send.at[i], recv_sem=kv_recv.at[i],
+            device_id=(sib, m), device_id_type=MESH)
+
+    def a_copy(p, k):
+        place = att.at[m * pairs + p]
+        return pltpu.make_async_remote_copy(
+            src_ref=place, dst_ref=place,
+            send_sem=a_send.at[p, k], recv_sem=a_recv.at[p, k],
+            device_id=(g, peers[k]), device_id_type=MESH)
+
+    tiles = rs_send.shape[0]
+    tile = rs_send.shape[2]
+
+    def r_copy(n, k):
+        return pltpu.make_async_remote_copy(
+            src_ref=rs_send.at[n, pl.ds(pl.multiple_of(peers[k] * share, share), share)],
+            dst_ref=rs_recv.at[k, n],
+            send_sem=r_send.at[n, k], recv_sem=r_recv.at[n, k],
+            device_id=(g, peers[k]), device_id_type=MESH)
+
+    def stage(kind):
+        if kind == Q:
+            for d in range(shards):
+                for j in range(3):
+                    stage_q[d, :, j * lw:(j + 1) * lw] = w_qkv[
+                        :, j * width + d * lw:j * width + (d + 1) * lw].astype(b16)
+        elif kind == O:
+            stage_o[0] = w_out[...].astype(b16)
+        else:
+            source = w_up if kind == U else w_down
+            for d in range(shards):
+                stages[kind][d] = source[:, d * lh:(d + 1) * lh].astype(b16)
+        fulls[kind][mine] = stages[kind][0 if kind == O else m]
+
+    stage(Q)
+    barrier = pltpu.get_barrier_semaphore()
+    everyone = [(g, peer) for peer in peers] + [(gx, m), (gy, m), (sib, m)]
+    for target in everyone:
+        pl.semaphore_signal(barrier, inc=1, device_id=target, device_id_type=MESH)
+    pl.semaphore_wait(barrier, len(everyone))
+    for kind in (Q, O, U, W):
+        if kind != Q:
+            stage(kind)
+        for k in range(shards - 1):
+            z_copy(kind, k).start()
+
+    long_id = jnp.where(core == 0, id_col[rows - 1:rows, :], id_col[0:1, :])
+    bias[:, :rows] = jnp.where(id_col[...] == id_row[...], 0.0, -1e30).astype(f32)
+    slot = sib * rows + lax.broadcasted_iota(jnp.int32, (1, rows), 1)
+    reach = jnp.where((slot > long_id - rows) & (slot <= long_id), long_id, -1)
+    bias[:, rows:] = jnp.where(id_col[...] == reach, 0.0, -1e30).astype(f32)
+
+    first_hop(Q)
+    second_hop(Q)
+    first_hop(O)
+    third_hop(Q)
+    finish(Q)
+
+    def project(j):
+        return jnp.dot(
+            hid[...], full_q[:, :, j * lw:(j + 1) * lw].reshape(width, lw),
+            preferred_element_type=f32).astype(b16)
+
+    key_rows = project(1)
+    keys[0] = key_rows
+    kv_copy(keys, 0).start()
+    k_out[...] = key_rows
+    value_rows = project(2)
+    vals[0] = value_rows
+    kv_copy(vals, 1).start()
+    v_out[...] = value_rows
+    queries[...] = project(0) * jnp.asarray(HD ** -0.5, b16)
+    first_hop(U)
+    kv_copy(keys, 0).wait_recv()
+    kv_copy(vals, 1).wait_recv()
+
+    q_tile = min(128, rows)
+    lane = lax.broadcasted_iota(jnp.int32, (q_tile, 128), 1)
+
+    def attend(p):
+        cols = slice(p * 128, (p + 1) * 128)
+        pair_keys = keys[:, :, cols].reshape(2 * rows, 128)
+        pair_vals = jnp.concatenate(
+            [vals[:, :, cols].reshape(2 * rows, 128), jnp.ones((2 * rows, 128), b16)], axis=1)
+
+        def step(i, carry):
+            here = pl.ds(pl.multiple_of(i * q_tile, q_tile), q_tile)
+            pair_q = queries[here, cols]
+            mask = bias[here, :]
+            halves = []
+            for h in range(2):
+                own = (lane < HD) if h == 0 else (lane >= HD)
+                head_q = jnp.where(own, pair_q, jnp.zeros_like(pair_q))
+                scores = lax.dot_general(
+                    head_q, pair_keys, (((1,), (1,)), ((), ())), preferred_element_type=f32) + mask
+                peak = jnp.max(scores, axis=-1, keepdims=True)
+                weights = jnp.exp(scores - peak).astype(b16)
+                mixed = jnp.dot(weights, pair_vals, preferred_element_type=f32)
+                halves.append(mixed[:, :128] / mixed[:, 128:])
+            att[m * pairs + p, here, :] = jnp.where(lane < HD, halves[0], halves[1]).astype(b16)
+            return carry
+
+        lax.fori_loop(0, rows // q_tile, step, 0)
+        for k in range(shards - 1):
+            a_copy(p, k).start()
+
+    attend(0)
+    second_hop(O)
+    for p in range(1, pairs):
+        attend(p)
+    third_hop(O)
+    first_hop(W)
+    second_hop(U)
+    third_hop(U)
+    second_hop(W)
+    finish(O)
+    for p in range(pairs):
+        for k in range(shards - 1):
+            a_copy(p, k).wait_recv()
+
+    n_wide = 256
+    o_parts = n_wide // part
+    joined = jnp.concatenate([att[i] for i in range(shards * pairs)], axis=1)
+
+    def out_step(n, carry):
+        block = full_o[pl.ds(n * o_parts, o_parts)].reshape(n_wide, width)
+        sums[:, pl.ds(pl.multiple_of(n * n_wide, n_wide), n_wide)] = lax.dot_general(
+            joined, block, (((1,), (1,)), ((), ())), preferred_element_type=f32)
+        return carry
+
+    lax.fori_loop(0, width // n_wide, out_step, 0)
+    ln_tile = 64
+
+    def ln_step(i, carry):
+        here = pl.ds(pl.multiple_of(i * ln_tile, ln_tile), ln_tile)
+        normed[here, :] = layer_norm(
+            hid[here, :].astype(f32) + sums[here, :], gain1[...], shift1[...]).astype(b16)
+        return carry
+
+    lax.fori_loop(0, rows // ln_tile, ln_step, 0)
+    third_hop(W)
+    finish(U)
+
+    def up_step(n, carry):
+        here = pl.ds(pl.multiple_of(n * n_wide, n_wide), n_wide)
+        pre = jnp.dot(
+            normed[...], full_u[:, :, here].reshape(width, n_wide), preferred_element_type=f32)
+        act[:, here] = (0.5 * pre * (1.0 + lax.erf(pre * (0.5 ** 0.5)))).astype(b16)
+        return carry
+
+    lax.fori_loop(0, lh // n_wide, up_step, 0)
+    finish(W)
+    d_parts = tile // part
+    for n in range(tiles):
+        block = full_d[n * d_parts:(n + 1) * d_parts].reshape(tile, lh)
+        term = lax.dot_general(
+            act[...], block, (((1,), (1,)), ((), ())), preferred_element_type=f32)
+        rs_send[n] = term.astype(b16)
+        for k in range(shards - 1):
+            r_copy(n, k).start()
+        sums[:, n * tile:(n + 1) * tile] = term
+    own_rows = pl.ds(pl.multiple_of(m * share, share), share)
+    for n in range(tiles):
+        cols = slice(n * tile, (n + 1) * tile)
+        total = normed[own_rows, cols].astype(f32) + sums[own_rows, cols]
+        for k in range(shards - 1):
+            r_copy(n, k).wait_recv()
+            total = total + rs_recv[k, n].astype(f32)
+        sums[0:share, cols] = total
+    out[...] = layer_norm(sums[0:share, :], gain2[...], shift2[...]).astype(b16)
+
+    for kind in (Q, O, U, W):
+        for k in range(shards - 1):
+            z_copy(kind, k).wait_send()
+        for step in range(len(hops)):
+            p_copy(kind, step).wait_send()
+    kv_copy(keys, 0).wait_send()
+    kv_copy(vals, 1).wait_send()
+    for k in range(shards - 1):
+        for p in range(pairs):
+            a_copy(p, k).wait_send()
+        for n in range(tiles):
+            r_copy(n, k).wait_send()
+
+
+def kernel_body(
+    hidden_in, request_ids, w_qkv, w_out, w_up, w_down, ln1_gain, ln1_shift, ln2_gain, ln2_shift
+):
+    groups = lax.axis_size("group")
+    shards = lax.axis_size("mp")
+    rows, width = hidden_in.shape
+    part = w_qkv.shape[0]
+    parts = groups * shards
+    lw = width // shards
+    lh = w_up.shape[1] // shards
+    share = rows // shards
+    pairs = lw // 128
+    tile = 256
+    tiles = width // tile
+    b16, f32 = jnp.bfloat16, jnp.float32
+    vmem = pl.BlockSpec(memory_space=pltpu.VMEM)
+    dma = pltpu.SemaphoreType.DMA
+    others = shards - 1
+    return pl.pallas_call(
+        functools.partial(layer_kernel, shards),
+        out_shape=(
+            jax.ShapeDtypeStruct((share, width), b16),
+            jax.ShapeDtypeStruct((rows, lw), b16),
+            jax.ShapeDtypeStruct((rows, lw), b16),
+        ),
+        in_specs=[vmem] * 11,
+        out_specs=(vmem,) * 3,
+        scratch_shapes=[
+            pltpu.VMEM((shards, part, 3 * lw), b16),
+            pltpu.VMEM((1, part, width), b16),
+            pltpu.VMEM((shards, part, lh), b16),
+            pltpu.VMEM((shards, part, lh), b16),
+            pltpu.VMEM((parts, part, 3 * lw), b16),
+            pltpu.VMEM((parts, part, width), b16),
+            pltpu.VMEM((parts, part, lh), b16),
+            pltpu.VMEM((parts, part, lh), b16),
+            pltpu.VMEM((rows, 2 * rows), f32),
+            pltpu.VMEM((rows, lw), b16),
+            pltpu.VMEM((2, rows, lw), b16),
+            pltpu.VMEM((2, rows, lw), b16),
+            pltpu.VMEM((shards * pairs, rows, 128), b16),
+            pltpu.VMEM((rows, width), f32),
+            pltpu.VMEM((rows, width), b16),
+            pltpu.VMEM((rows, lh), b16),
+            pltpu.VMEM((tiles, rows, tile), b16),
+            pltpu.VMEM((others, tiles, share, tile), b16),
+            dma((4, others)), dma((4, others)),
+            dma((4, 7)), dma((4, 7)),
+            dma((2,)), dma((2,)),
+            dma((pairs, others)), dma((pairs, others)),
+            dma((tiles, others)), dma((tiles, others)),
+        ],
+        compiler_params=pltpu.CompilerParams(
+            collective_id=0, has_side_effects=True, vmem_limit_bytes=48 * 1024 * 1024),
+        cost_estimate=pl.CostEstimate(
+            flops=6 * rows * width * (4 * lw + 2 * lh), bytes_accessed=16 * 1024 * 1024,
+            transcendentals=0),
+        name="encoder_layer",
+    )(
+        hidden_in, request_ids.reshape(rows, 1), request_ids.reshape(1, rows),
+        w_qkv, w_out, w_up, w_down,
+        ln1_gain.reshape(1, width), ln1_shift.reshape(1, width),
+        ln2_gain.reshape(1, width), ln2_shift.reshape(1, width),
+    )
+
+
 def solution(mesh):
     in_specs = (
         P("group", None),
@@ -179,4 +507,6 @@
         P(),
     )
     out_specs = (P(("group", "mp"), None), P("group", "mp"), P("group", "mp"))
+    whole_tiles = mesh.shape["group"] == 8 and mesh.shape["mp"] == 4
+    body = kernel_body if whole_tiles else plain_body
     return jax.shard_map(body, mesh=mesh, in_specs=in_specs, out_specs=out_specs, check_vma=False)

time: 375 us -> 94.5 us (0.25)
  the two profiles are of different devices: /device:TPU:21 before, /device:TPU:0 now
where the time goes in v1:
time: 94.5 us; the launch traced here: 94.1 us
  Pallas kernels  85.5 us (90%)
  local copies, waits for them, and re-layouts  7.97 us (8%)
    pallas_call x1, Pallas kernels, kernel_body(): pl.pallas_call(functools.partial(layer_kernel, shards), out_shape=(jax.Sh...  85.5 us
    unnamed x23, local copies, waits for them, and re-layouts  7.83 us

profile of v1, /device:TPU:0, one launch (start us, length us, event | category | flops | bytes accessed | tf_op | source)
XLA Modules:
  0.0 94.1 jit_solution(3985041535274071058)
XLA Ops:
  0.6 0.0 copy-start
  0.6 0.7 copy-done
  1.3 0.0 copy-start.5
  1.3 0.0 copy-start.6
  1.3 0.0 copy-start.7
  1.3 0.0 copy-start.8
  1.3 0.0 copy-start.9
  1.3 0.1 copy.13.id_col
  1.5 0.7 copy-done.5
  2.2 0.0 copy-done.6
  2.2 0.0 copy-done.7
  2.2 0.0 copy-done.8
  2.2 0.0 copy-done.9
  2.2 0.0 copy-start.1
  2.2 1.2 %copy-done.1 = bf16[512,1024]{1,0:T(8,128)(2,1)S(1)} copy-done((bf16[512,1024]{1,0:T(8,128)(2,1)S(1)}, bf16[512,1024]{1,0:T(8,128)(2,1)}, u32[]{:S(2)}) %copy-start.1) | copy-done | bytes 1048600
  3.5 0.0 copy-start.2
  3.5 1.0 %copy-done.2 = f32[32,4096]{1,0:T(8,128)S(1)} copy-done((f32[32,4096]{1,0:T(8,128)S(1)}, f32[32,4096]{1,0:T(8,128)}, u32[]{:S(2)}) %copy-start.2) | copy-done | bytes 524312
  4.5 0.0 copy-start.3
  4.5 1.0 %copy-done.3 = f32[32,4096]{1,0:T(8,128)S(1)} copy-done((f32[32,4096]{1,0:T(8,128)S(1)}, f32[32,4096]{1,0:T(8,128)}, u32[]{:S(2)}) %copy-start.3) | copy-done | bytes 524312
  5.5 0.0 copy-start.4
  5.5 1.0 %copy-done.4 = f32[32,3072]{1,0:T(8,128)S(1)} copy-done((f32[32,3072]{1,0:T(8,128)S(1)}, f32[32,3072]{1,0:T(8,128)}, u32[]{:S(2)}) %copy-start.4) | copy-done | bytes 393240
  6.5 85.5 %encoder_layer.1 = (bf16[128,1024]{1,0:T(8,128)(2,1)S(1)}, bf16[512,256]{1,0:T(8,128)(2,1)S(1)}, bf16[512,256]{1,0:T(8,128)(2,1)S(1)}) custom-call(bf16[512,1024]{1,0:T(8,128)(2,1)S(1)} %copy-done.1, s32[512,1]{1,0:T(8,128)S(1)} %copy.13.id_col, s32[1,512]{1,0:T(1,128)S(1)} %bitcast.7, f32[32,3072]{1,0:T(8,128)S(1)} %copy-done.4, f32[32,1024]{1,0:T(8,128)S(1)} %copy-done.5, ...), custom_call_target="tpu_custom_call" | custom-call | flops 9663676416 | bytes 16777216 | tf_op jit(solution)/shard_map/encoder_layer/pallas_call | solution.py:448
  92.0 0.7 copy.17
  92.7 0.7 copy.18
  93.4 0.7 copy.19
Async XLA Ops:
  0.6 0.7 copy-start
  1.3 0.9 copy-start.5
  1.3 0.9 copy-start.6
  1.3 0.9 copy-start.7
  1.3 0.9 copy-start.8
  1.3 0.9 copy-start.9
  2.2 1.2 %copy-start.1 = (bf16[512,1024]{1,0:T(8,128)(2,1)S(1)}, bf16[512,1024]{1,0:T(8,128)(2,1)}, u32[]{:S(2)}) copy-start(bf16[512,1024]{1,0:T(8,128)(2,1)} %hid.1) | copy-start | bytes 3145732
  3.5 1.0 %copy-start.2 = (f32[32,4096]{1,0:T(8,128)S(1)}, f32[32,4096]{1,0:T(8,128)}, u32[]{:S(2)}) copy-start(f32[32,4096]{1,0:T(8,128)} %w_up.1) | copy-start | bytes 1572868
  4.5 1.0 %copy-start.3 = (f32[32,4096]{1,0:T(8,128)S(1)}, f32[32,4096]{1,0:T(8,128)}, u32[]{:S(2)}) copy-start(f32[32,4096]{1,0:T(8,128)} %w_down.1) | copy-start | bytes 1572868
  5.5 1.0 %copy-start.4 = (f32[32,3072]{1,0:T(8,128)S(1)}, f32[32,3072]{1,0:T(8,128)}, u32[]{:S(2)}) copy-start(f32[32,3072]{1,0:T(8,128)} %w_qkv.1) | copy-start | bytes 1179652

commit v2 on v1

--- a/solution.py
+++ b/solution.py
@@ -174,19 +174,28 @@
 
 
 def layer_kernel(
-    shards, hid, id_col, id_row, w_qkv, w_out, w_up, w_down, gain1, shift1, gain2, shift2,
+    shards, hid_in, id_col, id_row, w_qkv_in, w_out_in, w_up_in, w_down_in,
+    gain1, shift1, gain2, shift2,
     out, k_out, v_out,
+    hid, w_qkv, w_out, w_up, w_down,
     stage_q, stage_o, stage_u, stage_d, full_q, full_o, full_u, full_d,
-    bias, queries, keys, vals, att, sums, normed, act, rs_send, rs_recv,
-    z_send, z_recv, p_send, p_recv, kv_send, kv_recv, a_send, a_recv, r_send, r_recv,
+    bias, queries, keys, vals, att, att_in, sums, normed, act, rs_send, rs_recv,
+    in_sem, z_send, z_recv, p_send, p_recv, kv_send, kv_recv, a_send, a_recv,
+    n_send, n_recv, r_send, r_recv,
 ):
     g = lax.axis_index("group")
     m = lax.axis_index("mp")
     core = lax.rem(g, 2)
+    x = lax.rem(g // 2, 2)
+    y = g // 4
+    half = m // 2
+    side = lax.rem(m, 2)
     sib = g + 1 - 2 * core
-    gx = g + 2 - 4 * lax.rem(g // 2, 2)
-    gy = g + 4 - 8 * (g // 4)
+    gx = g + 2 - 4 * x
+    gy = g + 4 - 8 * y
     gd = gx + gy - g
+    m1 = m + 1 - 2 * side
+    m2 = m + 2 - 4 * half
     rows = hid.shape[0]
     width = hid.shape[1]
     part = w_qkv.shape[0]
@@ -198,45 +207,58 @@
     fulls = (full_q, full_o, full_u, full_d)
     stages = (stage_q, stage_o, stage_u, stage_d)
     peers = [lax.rem(m + k, shards) for k in range(1, shards)]
-    mine = g * shards + m
+    spot = 2 * x + side
+    square = ((g, m1), (gx, m), (gx, m1))
+    square_spot = (2 * x + 1 - side, 2 - 2 * x + side, 3 - 2 * x - side)
+
+    def block_at(on_y, on_core, on_half):
+        return (on_y * 2 + on_core) * 2 + on_half
+
+    mine = (g * shards + m,) * 2 + (block_at(y, core, half) * 4 + spot,) * 2
 
     def z_copy(kind, k):
-        chunk = stages[kind].at[0] if kind == O else stages[kind].at[peers[k]]
+        if kind == Q:
+            chunk, target = stage_q.at[peers[k]], (g, peers[k])
+        elif kind == O:
+            chunk, target = stage_o.at[0], (g, peers[k])
+        else:
+            chunk, target = stages[kind].at[square_spot[k]], square[k]
         return pltpu.make_async_remote_copy(
-            src_ref=chunk, dst_ref=fulls[kind].at[mine],
+            src_ref=chunk, dst_ref=fulls[kind].at[mine[kind]],
             send_sem=z_send.at[kind, k], recv_sem=z_recv.at[kind, k],
-            device_id=(g, peers[k]), device_id_type=MESH)
+            device_id=target, device_id_type=MESH)
 
     fwd_to = gy * (1 - core) + gx * core
     fwd_block = gx * (1 - core) + gy * core
-    hops = ((g, gx), (g, gy), (fwd_block, fwd_to), (g, sib), (gx, sib), (gy, sib), (gd, sib))
+    plane_hops = (
+        (g, (gx, m)), (g, (gy, m)), (fwd_block, (fwd_to, m)),
+        (g, (sib, m)), (gx, (sib, m)), (gy, (sib, m)), (gd, (sib, m)))
+    b_own = block_at(y, core, half)
+    b_z = block_at(y, core, 1 - half)
+    b_y = block_at(1 - y, core, half)
+    b_d = block_at(1 - y, core, 1 - half)
+    hidden_hops = (
+        (b_own, (g, m2)), (b_own, (gy, m)), (b_z, (gy, m)),
+        (b_own, (sib, m)), (b_z, (sib, m)), (b_y, (sib, m)), (b_d, (sib, m)))
 
     def p_copy(kind, step):
-        block, target = hops[step]
-        place = fulls[kind].at[pl.ds(block * shards, shards)]
+        block, target = (plane_hops if kind in (Q, O) else hidden_hops)[step]
+        place = fulls[kind].at[pl.ds(block * 4, 4)]
         return pltpu.make_async_remote_copy(
             src_ref=place, dst_ref=place,
             send_sem=p_send.at[kind, step], recv_sem=p_recv.at[kind, step],
-            device_id=(target, m), device_id_type=MESH)
-
-    def first_hop(kind):
+            device_id=target, device_id_type=MESH)
+
+    def arrived(kind):
         for k in range(shards - 1):
             z_copy(kind, k).wait_recv()
-        for step in (0, 1, 3):
+
+    def go(kind, *steps):
+        for step in steps:
             p_copy(kind, step).start()
 
-    def second_hop(kind):
-        p_copy(kind, 0).wait_recv()
-        p_copy(kind, 1).wait_recv()
-        for step in (2, 4, 5):
-            p_copy(kind, step).start()
-
-    def third_hop(kind):
-        p_copy(kind, 2).wait_recv()
-        p_copy(kind, 6).start()
-
-    def finish(kind):
-        for step in (3, 4, 5, 6):
+    def landed(kind, *steps):
+        for step in steps:
             p_copy(kind, step).wait_recv()
 
     def kv_copy(buf, i):
@@ -246,23 +268,37 @@
             device_id=(sib, m), device_id_type=MESH)
 
     def a_copy(p, k):
-        place = att.at[m * pairs + p]
         return pltpu.make_async_remote_copy(
-            src_ref=place, dst_ref=place,
+            src_ref=att.at[p, pl.ds(pl.multiple_of(peers[k] * share, share), share)],
+            dst_ref=att_in.at[m * pairs + p],
             send_sem=a_send.at[p, k], recv_sem=a_recv.at[p, k],
             device_id=(g, peers[k]), device_id_type=MESH)
 
+    def n_copy(k):
+        return pltpu.make_async_remote_copy(
+            src_ref=normed.at[spot], dst_ref=normed.at[spot],
+            send_sem=n_send.at[k], recv_sem=n_recv.at[k],
+            device_id=square[k], device_id_type=MESH)
+
     tiles = rs_send.shape[0]
     tile = rs_send.shape[2]
 
     def r_copy(n, k):
         return pltpu.make_async_remote_copy(
-            src_ref=rs_send.at[n, pl.ds(pl.multiple_of(peers[k] * share, share), share)],
+            src_ref=rs_send.at[n, pl.ds(pl.multiple_of(square_spot[k] * share, share), share)],
             dst_ref=rs_recv.at[k, n],
             send_sem=r_send.at[n, k], recv_sem=r_recv.at[n, k],
-            device_id=(g, peers[k]), device_id_type=MESH)
+            device_id=square[k], device_id_type=MESH)
+
+    loads = [
+        pltpu.make_async_copy(far, near, in_sem.at[i])
+        for i, (far, near) in enumerate((
+            (w_qkv_in, w_qkv), (w_out_in, w_out), (w_up_in, w_up), (w_down_in, w_down),
+            (hid_in, hid)))
+    ]
 
     def stage(kind):
+        loads[kind].wait()
         if kind == Q:
             for d in range(shards):
                 for j in range(3):
@@ -274,15 +310,17 @@
             source = w_up if kind == U else w_down
             for d in range(shards):
                 stages[kind][d] = source[:, d * lh:(d + 1) * lh].astype(b16)
-        fulls[kind][mine] = stages[kind][0 if kind == O else m]
-
-    stage(Q)
+        fulls[kind][mine[kind]] = stages[kind][(m, 0, spot, spot)[kind]]
+
     barrier = pltpu.get_barrier_semaphore()
-    everyone = [(g, peer) for peer in peers] + [(gx, m), (gy, m), (sib, m)]
+    everyone = [(g, peer) for peer in peers] + [(gx, m), (gy, m), (sib, m), (gx, m1)]
     for target in everyone:
         pl.semaphore_signal(barrier, inc=1, device_id=target, device_id_type=MESH)
+    for load in loads:
+        load.start()
+    stage(Q)
     pl.semaphore_wait(barrier, len(everyone))
-    for kind in (Q, O, U, W):
+    for kind in (Q, U, O, W):
         if kind != Q:
             stage(kind)
         for k in range(shards - 1):
@@ -294,11 +332,20 @@
     reach = jnp.where((slot > long_id - rows) & (slot <= long_id), long_id, -1)
     bias[:, rows:] = jnp.where(id_col[...] == reach, 0.0, -1e30).astype(f32)
 
-    first_hop(Q)
-    second_hop(Q)
-    first_hop(O)
-    third_hop(Q)
-    finish(Q)
+    arrived(Q)
+    go(Q, 0, 1, 3)
+    arrived(U)
+    go(U, 0)
+    loads[4].wait()
+    landed(Q, 0, 1)
+    go(Q, 2, 4, 5)
+    arrived(O)
+    go(O, 0, 1, 3)
+    arrived(W)
+    go(W, 0)
+    landed(Q, 2)
+    go(Q, 6)
+    landed(Q, 3, 4, 5, 6)
 
     def project(j):
         return jnp.dot(
@@ -314,12 +361,13 @@
     kv_copy(vals, 1).start()
     v_out[...] = value_rows
     queries[...] = project(0) * jnp.asarray(HD ** -0.5, b16)
-    first_hop(U)
+    go(U, 1, 3)
     kv_copy(keys, 0).wait_recv()
     kv_copy(vals, 1).wait_recv()
 
     q_tile = min(128, rows)
     lane = lax.broadcasted_iota(jnp.int32, (q_tile, 128), 1)
+    own_rows = pl.ds(pl.multiple_of(m * share, share), share)
 
     def attend(p):
         cols = slice(p * 128, (p + 1) * 128)
@@ -341,73 +389,82 @@
                 weights = jnp.exp(scores - peak).astype(b16)
                 mixed = jnp.dot(weights, pair_vals, preferred_element_type=f32)
                 halves.append(mixed[:, :128] / mixed[:, 128:])
-            att[m * pairs + p, here, :] = jnp.where(lane < HD, halves[0], halves[1]).astype(b16)
+            att[p, here, :] = jnp.where(lane < HD, halves[0], halves[1]).astype(b16)
             return carry
 
         lax.fori_loop(0, rows // q_tile, step, 0)
         for k in range(shards - 1):
             a_copy(p, k).start()
+        att_in[m * pairs + p] = att[p, own_rows, :]
 
     attend(0)
-    second_hop(O)
+    landed(O, 0, 1)
+    go(O, 2, 4, 5)
     for p in range(1, pairs):
         attend(p)
-    third_hop(O)
-    first_hop(W)
-    second_hop(U)
-    third_hop(U)
-    second_hop(W)
-    finish(O)
+    landed(O, 2)
+    go(O, 6)
+    go(W, 1, 3)
+    landed(U, 0, 1)
+    go(U, 2, 4, 5)
+    landed(O, 3, 4, 5, 6)
     for p in range(pairs):
         for k in range(shards - 1):
             a_copy(p, k).wait_recv()
 
     n_wide = 256
     o_parts = n_wide // part
-    joined = jnp.concatenate([att[i] for i in range(shards * pairs)], axis=1)
-
-    def out_step(n, carry):
-        block = full_o[pl.ds(n * o_parts, o_parts)].reshape(n_wide, width)
-        sums[:, pl.ds(pl.multiple_of(n * n_wide, n_wide), n_wide)] = lax.dot_general(
+    joined = jnp.concatenate([att_in[i] for i in range(shards * pairs)], axis=1)
+
+    for n in range(width // n_wide):
+        block = full_o[n * o_parts:(n + 1) * o_parts].reshape(n_wide, width)
+        sums[0:share, n * n_wide:(n + 1) * n_wide] = lax.dot_general(
             joined, block, (((1,), (1,)), ((), ())), preferred_element_type=f32)
-        return carry
-
-    lax.fori_loop(0, width // n_wide, out_step, 0)
-    ln_tile = 64
-
-    def ln_step(i, carry):
-        here = pl.ds(pl.multiple_of(i * ln_tile, ln_tile), ln_tile)
-        normed[here, :] = layer_norm(
-            hid[here, :].astype(f32) + sums[here, :], gain1[...], shift1[...]).astype(b16)
-        return carry
-
-    lax.fori_loop(0, rows // ln_tile, ln_step, 0)
-    third_hop(W)
-    finish(U)
+    normed[spot] = layer_norm(
+        hid[own_rows, :].astype(f32) + sums[0:share, :], gain1[...], shift1[...]).astype(b16)
+    for k in range(3):
+        n_copy(k).start()
+    landed(U, 2)
+    go(U, 6)
+    landed(W, 0, 1)
+    go(W, 2, 4, 5)
+    landed(U, 3, 4, 5, 6)
+    for k in range(3):
+        n_copy(k).wait_recv()
+
+    order = []
+    for r in range(8 * shards):
+        group_r, z_r = r // shards, r % shards
+        order.append(((group_r // 4 * 2 + group_r % 2) * 2 + z_r // 2) * 4
+                     + group_r // 2 % 2 * 2 + z_r % 2)
+    tokens = normed[...].reshape(rows, width)
 
     def up_step(n, carry):
         here = pl.ds(pl.multiple_of(n * n_wide, n_wide), n_wide)
-        pre = jnp.dot(
-            normed[...], full_u[:, :, here].reshape(width, n_wide), preferred_element_type=f32)
+        block = jnp.concatenate([full_u[r, :, here] for r in order], axis=0)
+        pre = jnp.dot(tokens, block, preferred_element_type=f32)
         act[:, here] = (0.5 * pre * (1.0 + lax.erf(pre * (0.5 ** 0.5)))).astype(b16)
         return carry
 
     lax.fori_loop(0, lh // n_wide, up_step, 0)
-    finish(W)
+    landed(W, 2)
+    go(W, 6)
+    landed(W, 3, 4, 5, 6)
     d_parts = tile // part
     for n in range(tiles):
-        block = full_d[n * d_parts:(n + 1) * d_parts].reshape(tile, lh)
+        block = jnp.concatenate(
+            [full_d[r] for r in order[n * d_parts:(n + 1) * d_parts]], axis=0)
         term = lax.dot_general(
             act[...], block, (((1,), (1,)), ((), ())), preferred_element_type=f32)
         rs_send[n] = term.astype(b16)
-        for k in range(shards - 1):
+        for k in range(3):
             r_copy(n, k).start()
         sums[:, n * tile:(n + 1) * tile] = term
-    own_rows = pl.ds(pl.multiple_of(m * share, share), share)
+    spot_rows = pl.ds(pl.multiple_of(spot * share, share), share)
     for n in range(tiles):
         cols = slice(n * tile, (n + 1) * tile)
-        total = normed[own_rows, cols].astype(f32) + sums[own_rows, cols]
-        for k in range(shards - 1):
+        total = normed[spot, :, cols].astype(f32) + sums[spot_rows, cols]
+        for k in range(3):
             r_copy(n, k).wait_recv()
             total = total + rs_recv[k, n].astype(f32)
         sums[0:share, cols] = total
@@ -416,11 +473,12 @@
     for kind in (Q, O, U, W):
         for k in range(shards - 1):
             z_copy(kind, k).wait_send()
-        for step in range(len(hops)):
+        for step in range(7):
             p_copy(kind, step).wait_send()
     kv_copy(keys, 0).wait_send()
     kv_copy(vals, 1).wait_send()
     for k in range(shards - 1):
+        n_copy(k).wait_send()
         for p in range(pairs):
             a_copy(p, k).wait_send()
         for n in range(tiles):
@@ -443,6 +501,7 @@
     tiles = width // tile
     b16, f32 = jnp.bfloat16, jnp.float32
     vmem = pl.BlockSpec(memory_space=pltpu.VMEM)
+    hbm = pl.BlockSpec(memory_space=pl.ANY)
     dma = pltpu.SemaphoreType.DMA
     others = shards - 1
     return pl.pallas_call(
@@ -452,9 +511,14 @@
             jax.ShapeDtypeStruct((rows, lw), b16),
             jax.ShapeDtypeStruct((rows, lw), b16),
         ),
-        in_specs=[vmem] * 11,
+        in_specs=[hbm] + [vmem] * 2 + [hbm] * 4 + [vmem] * 4,
         out_specs=(vmem,) * 3,
         scratch_shapes=[
+            pltpu.VMEM((rows, width), b16),
+            pltpu.VMEM(w_qkv.shape, f32),
+            pltpu.VMEM(w_out.shape, f32),
+            pltpu.VMEM(w_up.shape, f32),
+            pltpu.VMEM(w_down.shape, f32),
             pltpu.VMEM((shards, part, 3 * lw), b16),
             pltpu.VMEM((1, part, width), b16),
             pltpu.VMEM((shards, part, lh), b16),
@@ -467,16 +531,19 @@
             pltpu.VMEM((rows, lw), b16),
             pltpu.VMEM((2, rows, lw), b16),
             pltpu.VMEM((2, rows, lw), b16),
-            pltpu.VMEM((shards * pairs, rows, 128), b16),
+            pltpu.VMEM((pairs, rows, 128), b16),
+            pltpu.VMEM((shards * pairs, share, 128), b16),
             pltpu.VMEM((rows, width), f32),
-            pltpu.VMEM((rows, width), b16),
+            pltpu.VMEM((shards, share, width), b16),
             pltpu.VMEM((rows, lh), b16),
             pltpu.VMEM((tiles, rows, tile), b16),
             pltpu.VMEM((others, tiles, share, tile), b16),
+            dma((5,)),
             dma((4, others)), dma((4, others)),
             dma((4, 7)), dma((4, 7)),
             dma((2,)), dma((2,)),
             dma((pairs, others)), dma((pairs, others)),
+            dma((others,)), dma((others,)),
             dma((tiles, others)), dma((tiles, others)),
         ],
         compiler_params=pltpu.CompilerParams(

time: 94.5 us -> 85.4 us (0.904)
  the two profiles are of different devices: /device:TPU:0 before, /device:TPU:1 now
where the time goes in v2:
time: 85.4 us; the launch traced here: 85.1 us
  Pallas kernels  76.4 us (89%)
  local copies, waits for them, and re-layouts  7.97 us (9%)
    pallas_call x1, Pallas kernels, kernel_body(): pl.pallas_call(functools.partial(layer_kernel, shards), out_shape=(jax.Sh...  76.4 us
    unnamed x23, local copies, waits for them, and re-layouts  7.83 us

profile of v2, /device:TPU:1, one launch (start us, length us, event | category | flops | bytes accessed | tf_op | source)
XLA Modules:
  0.0 85.1 jit_solution(16722180115018530165)
XLA Ops:
  0.6 0.0 copy-start
  0.6 0.7 copy-done
  1.3 0.0 copy-start.5
  1.3 0.0 copy-start.6
  1.3 0.0 copy-start.7
  1.3 0.0 copy-start.8
  1.3 0.0 copy-start.9
  1.3 0.1 copy.13.id_col
  1.5 0.7 copy-done.5
  2.2 0.0 copy-done.6
  2.2 0.0 copy-done.7
  2.2 0.0 copy-done.8
  2.2 0.0 copy-done.9
  2.2 0.0 copy-start.1
  2.2 1.2 %copy-done.1 = bf16[512,1024]{1,0:T(8,128)(2,1)S(1)} copy-done((bf16[512,1024]{1,0:T(8,128)(2,1)S(1)}, bf16[512,1024]{1,0:T(8,128)(2,1)}, u32[]{:S(2)}) %copy-start.1) | copy-done | bytes 1048600
  3.5 0.0 copy-start.2
  3.5 1.0 %copy-done.2 = f32[32,4096]{1,0:T(8,128)S(1)} copy-done((f32[32,4096]{1,0:T(8,128)S(1)}, f32[32,4096]{1,0:T(8,128)}, u32[]{:S(2)}) %copy-start.2) | copy-done | bytes 524312
  4.5 0.0 copy-start.3
  4.5 1.0 %copy-done.3 = f32[32,4096]{1,0:T(8,128)S(1)} copy-done((f32[32,4096]{1,0:T(8,128)S(1)}, f32[32,4096]{1,0:T(8,128)}, u32[]{:S(2)}) %copy-start.3) | copy-done | bytes 524312
  5.5 0.0 copy-start.4
  5.5 1.0 %copy-done.4 = f32[32,3072]{1,0:T(8,128)S(1)} copy-done((f32[32,3072]{1,0:T(8,128)S(1)}, f32[32,3072]{1,0:T(8,128)}, u32[]{:S(2)}) %copy-start.4) | copy-done | bytes 393240
  6.5 76.4 %encoder_layer.1 = (bf16[128,1024]{1,0:T(8,128)(2,1)S(1)}, bf16[512,256]{1,0:T(8,128)(2,1)S(1)}, bf16[512,256]{1,0:T(8,128)(2,1)S(1)}) custom-call(bf16[512,1024]{1,0:T(8,128)(2,1)S(1)} %copy-done.1, s32[512,1]{1,0:T(8,128)S(1)} %copy.13.id_col, s32[1,512]{1,0:T(1,128)S(1)} %bitcast.7, f32[32,3072]{1,0:T(8,128)S(1)} %copy-done.4, f32[32,1024]{1,0:T(8,128)S(1)} %copy-done.5, ...), custom_call_target="tpu_custom_call" | custom-call | flops 9663676416 | bytes 16777216 | tf_op jit(solution)/shard_map/encoder_layer/pallas_call | solution.py:507
  82.9 0.7 copy.17
  83.6 0.7 copy.18
  84.3 0.7 copy.19
Async XLA Ops:
  0.6 0.7 copy-start
  1.3 0.9 %copy-start.5 = (f32[32,1024]{1,0:T(8,128)S(1)}, f32[32,1024]{1,0:T(8,128)}, u32[]{:S(2)}) copy-start(f32[32,1024]{1,0:T(8,128)} %w_out_in.1) | copy-start | bytes 393220
  1.3 0.9 %copy-start.6 = (f32[1024]{0:T(1024)S(1)}, f32[1024]{0:T(1024)}, u32[]{:S(2)}) copy-start(f32[1024]{0:T(1024)} %param.16) | copy-start | bytes 12292
  1.3 0.9 %copy-start.7 = (f32[1024]{0:T(1024)S(1)}, f32[1024]{0:T(1024)}, u32[]{:S(2)}) copy-start(f32[1024]{0:T(1024)} %param.17) | copy-start | bytes 12292
  1.3 0.9 %copy-start.8 = (f32[1024]{0:T(1024)S(1)}, f32[1024]{0:T(1024)}, u32[]{:S(2)}) copy-start(f32[1024]{0:T(1024)} %param.18) | copy-start | bytes 12292
  1.3 0.9 %copy-start.9 = (f32[1024]{0:T(1024)S(1)}, f32[1024]{0:T(1024)}, u32[]{:S(2)}) copy-start(f32[1024]{0:T(1024)} %param.19) | copy-start | bytes 12292
  2.2 1.2 %copy-start.1 = (bf16[512,1024]{1,0:T(8,128)(2,1)S(1)}, bf16[512,1024]{1,0:T(8,128)(2,1)}, u32[]{:S(2)}) copy-start(bf16[512,1024]{1,0:T(8,128)(2,1)} %hid_in.1) | copy-start | bytes 3145732
  3.5 1.0 %copy-start.2 = (f32[32,4096]{1,0:T(8,128)S(1)}, f32[32,4096]{1,0:T(8,128)}, u32[]{:S(2)}) copy-start(f32[32,4096]{1,0:T(8,128)} %w_up_in.1) | copy-start | bytes 1572868
  4.5 1.0 %copy-start.3 = (f32[32,4096]{1,0:T(8,128)S(1)}, f32[32,4096]{1,0:T(8,128)}, u32[]{:S(2)}) copy-start(f32[32,4096]{1,0:T(8,128)} %w_down_in.1) | copy-start | bytes 1572868
  5.5 1.0 %copy-start.4 = (f32[32,3072]{1,0:T(8,128)S(1)}, f32[32,3072]{1,0:T(8,128)}, u32[]{:S(2)}) copy-start(f32[32,3072]{1,0:T(8,128)} %w_qkv_in.1) | copy-start | bytes 1179652

commit v3 on v2

--- a/solution.py
+++ b/solution.py
@@ -200,7 +200,7 @@
     width = hid.shape[1]
     part = w_qkv.shape[0]
     lw = queries.shape[1]
-    lh = act.shape[1]
+    lh = act.shape[2]
     pairs = lw // 128
     share = rows // shards
     f32, b16 = jnp.float32, jnp.bfloat16
@@ -228,10 +228,8 @@
             send_sem=z_send.at[kind, k], recv_sem=z_recv.at[kind, k],
             device_id=target, device_id_type=MESH)
 
-    fwd_to = gy * (1 - core) + gx * core
-    fwd_block = gx * (1 - core) + gy * core
     plane_hops = (
-        (g, (gx, m)), (g, (gy, m)), (fwd_block, (fwd_to, m)),
+        (g, (gx, m)), (g, (gy, m)), (gy, (gx, m)),
         (g, (sib, m)), (gx, (sib, m)), (gy, (sib, m)), (gd, (sib, m)))
     b_own = block_at(y, core, half)
     b_z = block_at(y, core, 1 - half)
@@ -269,7 +267,7 @@
 
     def a_copy(p, k):
         return pltpu.make_async_remote_copy(
-            src_ref=att.at[p, pl.ds(pl.multiple_of(peers[k] * share, share), share)],
+            src_ref=att.at[p, k],
             dst_ref=att_in.at[m * pairs + p],
             send_sem=a_send.at[p, k], recv_sem=a_recv.at[p, k],
             device_id=(g, peers[k]), device_id_type=MESH)
@@ -280,12 +278,12 @@
             send_sem=n_send.at[k], recv_sem=n_recv.at[k],
             device_id=square[k], device_id_type=MESH)
 
-    tiles = rs_send.shape[0]
-    tile = rs_send.shape[2]
+    tiles = rs_send.shape[1]
+    tile = rs_send.shape[3]
 
     def r_copy(n, k):
         return pltpu.make_async_remote_copy(
-            src_ref=rs_send.at[n, pl.ds(pl.multiple_of(square_spot[k] * share, share), share)],
+            src_ref=rs_send.at[k, n],
             dst_ref=rs_recv.at[k, n],
             send_sem=r_send.at[n, k], recv_sem=r_recv.at[n, k],
             device_id=square[k], device_id_type=MESH)
@@ -320,11 +318,16 @@
         load.start()
     stage(Q)
     pl.semaphore_wait(barrier, len(everyone))
-    for kind in (Q, U, O, W):
-        if kind != Q:
-            stage(kind)
+
+    def depart(kind):
         for k in range(shards - 1):
             z_copy(kind, k).start()
+
+    depart(Q)
+    stage(U)
+    depart(U)
+    stage(O)
+    stage(W)
 
     long_id = jnp.where(core == 0, id_col[rows - 1:rows, :], id_col[0:1, :])
     bias[:, :rows] = jnp.where(id_col[...] == id_row[...], 0.0, -1e30).astype(f32)
@@ -334,15 +337,15 @@
 
     arrived(Q)
     go(Q, 0, 1, 3)
+    depart(O)
     arrived(U)
     go(U, 0)
+    depart(W)
     loads[4].wait()
     landed(Q, 0, 1)
     go(Q, 2, 4, 5)
     arrived(O)
     go(O, 0, 1, 3)
-    arrived(W)
-    go(W, 0)
     landed(Q, 2)
     go(Q, 6)
     landed(Q, 3, 4, 5, 6)
@@ -362,10 +365,12 @@
     v_out[...] = value_rows
     queries[...] = project(0) * jnp.asarray(HD ** -0.5, b16)
     go(U, 1, 3)
+    arrived(W)
+    go(W, 0)
     kv_copy(keys, 0).wait_recv()
     kv_copy(vals, 1).wait_recv()
 
-    q_tile = min(128, rows)
+    q_tile = share
     lane = lax.broadcasted_iota(jnp.int32, (q_tile, 128), 1)
     own_rows = pl.ds(pl.multiple_of(m * share, share), share)
 
@@ -375,8 +380,9 @@
         pair_vals = jnp.concatenate(
             [vals[:, :, cols].reshape(2 * rows, 128), jnp.ones((2 * rows, 128), b16)], axis=1)
 
-        def step(i, carry):
-            here = pl.ds(pl.multiple_of(i * q_tile, q_tile), q_tile)
+        for k in range(shards):
+            target = peers[k] if k < shards - 1 else m
+            here = pl.ds(pl.multiple_of(target * q_tile, q_tile), q_tile)
             pair_q = queries[here, cols]
             mask = bias[here, :]
             halves = []
@@ -389,13 +395,12 @@
                 weights = jnp.exp(scores - peak).astype(b16)
                 mixed = jnp.dot(weights, pair_vals, preferred_element_type=f32)
                 halves.append(mixed[:, :128] / mixed[:, 128:])
-            att[p, here, :] = jnp.where(lane < HD, halves[0], halves[1]).astype(b16)
-            return carry
-
-        lax.fori_loop(0, rows // q_tile, step, 0)
-        for k in range(shards - 1):
-            a_copy(p, k).start()
-        att_in[m * pairs + p] = att[p, own_rows, :]
+            mixed_rows = jnp.where(lane < HD, halves[0], halves[1]).astype(b16)
+            if k < shards - 1:
+                att[p, k] = mixed_rows
+                a_copy(p, k).start()
+            else:
+                att_in[m * pairs + p] = mixed_rows
 
     attend(0)
     landed(O, 0, 1)
@@ -418,57 +423,70 @@
 
     for n in range(width // n_wide):
         block = full_o[n * o_parts:(n + 1) * o_parts].reshape(n_wide, width)
-        sums[0:share, n * n_wide:(n + 1) * n_wide] = lax.dot_general(
+        sums[:, n * n_wide:(n + 1) * n_wide] = lax.dot_general(
             joined, block, (((1,), (1,)), ((), ())), preferred_element_type=f32)
     normed[spot] = layer_norm(
-        hid[own_rows, :].astype(f32) + sums[0:share, :], gain1[...], shift1[...]).astype(b16)
-    for k in range(3):
+        hid[own_rows, :].astype(f32) + sums[...], gain1[...], shift1[...]).astype(b16)
+    for k in (1, 0, 2):
         n_copy(k).start()
     landed(U, 2)
     go(U, 6)
     landed(W, 0, 1)
     go(W, 2, 4, 5)
     landed(U, 3, 4, 5, 6)
-    for k in range(3):
-        n_copy(k).wait_recv()
 
     order = []
     for r in range(8 * shards):
         group_r, z_r = r // shards, r % shards
         order.append(((group_r // 4 * 2 + group_r % 2) * 2 + z_r // 2) * 4
                      + group_r // 2 % 2 * 2 + z_r % 2)
-    tokens = normed[...].reshape(rows, width)
-
-    def up_step(n, carry):
-        here = pl.ds(pl.multiple_of(n * n_wide, n_wide), n_wide)
-        block = jnp.concatenate([full_u[r, :, here] for r in order], axis=0)
-        pre = jnp.dot(tokens, block, preferred_element_type=f32)
-        act[:, here] = (0.5 * pre * (1.0 + lax.erf(pre * (0.5 ** 0.5)))).astype(b16)
-        return carry
-
-    lax.fori_loop(0, lh // n_wide, up_step, 0)
+    d_parts = tile // part
+
+    def up(batch, spots):
+        tokens = jnp.concatenate([normed[i] for i in spots], axis=0)
+
+        def up_step(n, carry):
+            here = pl.ds(pl.multiple_of(n * n_wide, n_wide), n_wide)
+            block = jnp.concatenate([full_u[r, :, here] for r in order], axis=0)
+            pre = jnp.dot(tokens, block, preferred_element_type=f32)
+            act[batch, :, here] = (0.5 * pre * (1.0 + lax.erf(pre * (0.5 ** 0.5)))).astype(b16)
+            return carry
+
+        lax.fori_loop(0, lh // n_wide, up_step, 0)
+
+    def down(batch, n):
+        block = jnp.concatenate(
+            [full_d[r] for r in order[n * d_parts:(n + 1) * d_parts]], axis=0)
+        return lax.dot_general(
+            act[batch], block, (((1,), (1,)), ((), ())), preferred_element_type=f32)
+
+    n_copy(1).wait_recv()
+    up(0, (spot, square_spot[1]))
     landed(W, 2)
     go(W, 6)
     landed(W, 3, 4, 5, 6)
-    d_parts = tile // part
     for n in range(tiles):
-        block = jnp.concatenate(
-            [full_d[r] for r in order[n * d_parts:(n + 1) * d_parts]], axis=0)
-        term = lax.dot_general(
-            act[...], block, (((1,), (1,)), ((), ())), preferred_element_type=f32)
-        rs_send[n] = term.astype(b16)
-        for k in range(3):
-            r_copy(n, k).start()
-        sums[:, n * tile:(n + 1) * tile] = term
-    spot_rows = pl.ds(pl.multiple_of(spot * share, share), share)
+        term = down(0, n)
+        rs_send[1, n] = term[share:].astype(b16)
+        r_copy(n, 1).start()
+        sums[:, n * tile:(n + 1) * tile] = term[:share]
+    n_copy(0).wait_recv()
+    n_copy(2).wait_recv()
+    up(1, (square_spot[2], square_spot[0]))
+    for n in range(tiles):
+        term = down(1, n)
+        rs_send[2, n] = term[:share].astype(b16)
+        r_copy(n, 2).start()
+        rs_send[0, n] = term[share:].astype(b16)
+        r_copy(n, 0).start()
     for n in range(tiles):
         cols = slice(n * tile, (n + 1) * tile)
-        total = normed[spot, :, cols].astype(f32) + sums[spot_rows, cols]
-        for k in range(3):
+        total = normed[spot, :, cols].astype(f32) + sums[:, cols]
+        for k in (1, 0, 2):
             r_copy(n, k).wait_recv()
             total = total + rs_recv[k, n].astype(f32)
-        sums[0:share, cols] = total
-    out[...] = layer_norm(sums[0:share, :], gain2[...], shift2[...]).astype(b16)
+        sums[:, cols] = total
+    out[...] = layer_norm(sums[...], gain2[...], shift2[...]).astype(b16)
 
     for kind in (Q, O, U, W):
         for k in range(shards - 1):
@@ -501,7 +519,7 @@
     tiles = width // tile
     b16, f32 = jnp.bfloat16, jnp.float32
     vmem = pl.BlockSpec(memory_space=pltpu.VMEM)
-    hbm = pl.BlockSpec(memory_space=pl.ANY)
+    hbm = pl.BlockSpec(memory_space=pltpu.HBM)
     dma = pltpu.SemaphoreType.DMA
     others = shards - 1
     return pl.pallas_call(
@@ -531,12 +549,12 @@
             pltpu.VMEM((rows, lw), b16),
             pltpu.VMEM((2, rows, lw), b16),
             pltpu.VMEM((2, rows, lw), b16),
-            pltpu.VMEM((pairs, rows, 128), b16),
+            pltpu.VMEM((pairs, others, share, 128), b16),
             pltpu.VMEM((shards * pairs, share, 128), b16),
-            pltpu.VMEM((rows, width), f32),
+            pltpu.VMEM((share, width), f32),
             pltpu.VMEM((shards, share, width), b16),
-            pltpu.VMEM((rows, lh), b16),
-            pltpu.VMEM((tiles, rows, tile), b16),
+            pltpu.VMEM((2, rows // 2, lh), b16),
+            pltpu.VMEM((others, tiles, share, tile), b16),
             pltpu.VMEM((others, tiles, share, tile), b16),
             dma((5,)),
             dma((4, others)), dma((4, others)),
@@ -547,7 +565,7 @@
             dma((tiles, others)), dma((tiles, others)),
         ],
         compiler_params=pltpu.CompilerParams(
-            collective_id=0, has_side_effects=True, vmem_limit_bytes=48 * 1024 * 1024),
+            collective_id=0, has_side_effects=True, vmem_limit_bytes=60 * 1024 * 1024),
         cost_estimate=pl.CostEstimate(
             flops=6 * rows * width * (4 * lw + 2 * lh), bytes_accessed=16 * 1024 * 1024,
             transcendentals=0),

time: 85.4 us -> 86.1 us (level)
  the two profiles are of different devices: /device:TPU:1 before, /device:TPU:21 now
where the time goes in v3:
time: 86.1 us; the launch traced here: 85.8 us
  Pallas kernels  80.2 us (93%)
  local copies, waits for them, and re-layouts  5 us (6%)
    pallas_call x1, Pallas kernels, kernel_body(): pl.pallas_call(functools.partial(layer_kernel, shards), out_shape=(jax.Sh...  80.2 us
    unnamed x9, local copies, waits for them, and re-layouts  4.14 us

profile of v3, /device:TPU:21, one launch (start us, length us, event | category | flops | bytes accessed | tf_op | source)
XLA Modules:
  0.0 85.8 jit_solution(11545291601574344435)
XLA Ops:
  0.6 0.0 copy-start.2
  0.6 0.7 copy-done.2
  1.3 0.9 %copy.13.id_col = s32[512,1]{1,0:T(8,128)} copy(s32[512,1]{0,1:T(1,128)S(1)} %bitcast.7) | data formatting | bytes 4096 | tf_op jit(solution)/shard_map/reshape | solution.py:574
  2.2 80.2 %encoder_layer.1 = (bf16[128,1024]{1,0:T(8,128)(2,1)}, bf16[512,256]{1,0:T(8,128)(2,1)}, bf16[512,256]{1,0:T(8,128)(2,1)}) custom-call(bf16[512,1024]{1,0:T(8,128)(2,1)} %hid_in.1, s32[512,1]{1,0:T(8,128)} %copy.13.id_col, s32[1,512]{1,0:T(1,128)} %bitcast.6, f32[32,3072]{1,0:T(8,128)} %w_qkv_in.1, f32[32,1024]{1,0:T(8,128)} %w_out_in.1, ...), custom_call_target="tpu_custom_call" | custom-call | flops 9663676416 | bytes 16777216 | tf_op jit(solution)/shard_map/encoder_layer/pallas_call | solution.py:525
  82.3 0.0 copy-start.1
  82.4 1.7 %copy.17 = bf16[128,1024]{1,0:T(8,128)(2,1)} copy(bf16[128,1024]{1,0:T(8,128)(2,1)} %get-tuple-element.6) | data formatting | bytes 524288
  84.1 0.0 copy-done.1
  84.1 0.0 copy-start
  84.1 0.7 copy.18
  84.8 0.3 copy-done
  85.1 0.7 copy.19
Async XLA Ops:
  0.6 0.7 copy-start.2
  82.3 1.7 %copy-start.1 = (bf16[512,256]{1,0:T(8,128)(2,1)S(1)}, bf16[512,256]{1,0:T(8,128)(2,1)}, u32[]{:S(2)}) copy-start(bf16[512,256]{1,0:T(8,128)(2,1)} %get-tuple-element.7) | copy-start | bytes 786436
  84.1 1.0 %copy-start = (bf16[512,256]{1,0:T(8,128)(2,1)S(1)}, bf16[512,256]{1,0:T(8,128)(2,1)}, u32[]{:S(2)}) copy-start(bf16[512,256]{1,0:T(8,128)(2,1)} %get-tuple-element.8) | copy-start | bytes 786436

commit v4 on v3

--- a/solution.py
+++ b/solution.py
@@ -179,7 +179,7 @@
     out, k_out, v_out,
     hid, w_qkv, w_out, w_up, w_down,
     stage_q, stage_o, stage_u, stage_d, full_q, full_o, full_u, full_d,
-    bias, queries, keys, vals, att, att_in, sums, normed, act, rs_send, rs_recv,
+    bias, queries, kv, vals_ones, att, att_in, sums, normed, act, rs_send, rs_recv,
     in_sem, z_send, z_recv, p_send, p_recv, kv_send, kv_recv, a_send, a_recv,
     n_send, n_recv, r_send, r_recv,
 ):
@@ -200,7 +200,7 @@
     width = hid.shape[1]
     part = w_qkv.shape[0]
     lw = queries.shape[1]
-    lh = act.shape[2]
+    lh = act.shape[1]
     pairs = lw // 128
     share = rows // shards
     f32, b16 = jnp.float32, jnp.bfloat16
@@ -259,9 +259,9 @@
         for step in steps:
             p_copy(kind, step).wait_recv()
 
-    def kv_copy(buf, i):
+    def kv_copy(i):
         return pltpu.make_async_remote_copy(
-            src_ref=buf.at[0], dst_ref=buf.at[1],
+            src_ref=kv.at[i, 0], dst_ref=kv.at[i, 1],
             send_sem=kv_send.at[i], recv_sem=kv_recv.at[i],
             device_id=(sib, m), device_id_type=MESH)
 
@@ -270,7 +270,7 @@
             src_ref=att.at[p, k],
             dst_ref=att_in.at[m * pairs + p],
             send_sem=a_send.at[p, k], recv_sem=a_recv.at[p, k],
-            device_id=(g, peers[k]), device_id_type=MESH)
+            device_id=(g, lax.rem(m + 1 + k, shards)), device_id_type=MESH)
 
     def n_copy(k):
         return pltpu.make_async_remote_copy(
@@ -330,10 +330,21 @@
     stage(W)
 
     long_id = jnp.where(core == 0, id_col[rows - 1:rows, :], id_col[0:1, :])
-    bias[:, :rows] = jnp.where(id_col[...] == id_row[...], 0.0, -1e30).astype(f32)
     slot = sib * rows + lax.broadcasted_iota(jnp.int32, (1, rows), 1)
     reach = jnp.where((slot > long_id - rows) & (slot <= long_id), long_id, -1)
-    bias[:, rows:] = jnp.where(id_col[...] == reach, 0.0, -1e30).astype(f32)
+    few = 32
+
+    def bias_step(i, carry):
+        here = pl.ds(pl.multiple_of(i * few, few), few)
+        ids = id_col[here, :]
+        bias[here, :rows] = jnp.where(ids == id_row[...], 0.0, -1e30).astype(f32)
+        bias[here, rows:] = jnp.where(ids == reach, 0.0, -1e30).astype(f32)
+        return carry
+
+    lax.fori_loop(0, rows // few, bias_step, 0)
+    for p in range(pairs):
+        for i in range(2):
+            vals_ones[p, i, :, 128:] = jnp.ones((rows, 128), b16)
 
     arrived(Q)
     go(Q, 0, 1, 3)
@@ -350,68 +361,84 @@
     go(Q, 6)
     landed(Q, 3, 4, 5, 6)
 
-    def project(j):
-        return jnp.dot(
-            hid[...], full_q[:, :, j * lw:(j + 1) * lw].reshape(width, lw),
-            preferred_element_type=f32).astype(b16)
-
-    key_rows = project(1)
-    keys[0] = key_rows
-    kv_copy(keys, 0).start()
-    k_out[...] = key_rows
-    value_rows = project(2)
-    vals[0] = value_rows
-    kv_copy(vals, 1).start()
-    v_out[...] = value_rows
-    queries[...] = project(0) * jnp.asarray(HD ** -0.5, b16)
+    def project(i, carry):
+        j = lax.rem(i + 1, 3)
+        here = pl.ds(pl.multiple_of(j * lw, lw), lw)
+        block = full_q[:, :, here].reshape(width, lw)
+        some = jnp.dot(hid[...], block, preferred_element_type=f32).astype(b16)
+
+        @pl.when(i < 2)
+        def _():
+            kv[i, 0] = some
+            kv_copy(i).start()
+
+        @pl.when(i == 2)
+        def _():
+            queries[...] = some * jnp.asarray(HD ** -0.5, b16)
+
+        return carry
+
+    lax.fori_loop(0, 3, project, 0)
     go(U, 1, 3)
     arrived(W)
-    go(W, 0)
-    kv_copy(keys, 0).wait_recv()
-    kv_copy(vals, 1).wait_recv()
-
-    q_tile = share
-    lane = lax.broadcasted_iota(jnp.int32, (q_tile, 128), 1)
+    go(W, 0, 1, 3)
+    k_out[...] = kv[0, 0]
+    v_out[...] = kv[1, 0]
+    for i in range(2):
+        kv_copy(i).wait_recv()
+    for p in range(pairs):
+        vals_ones[p, :, :, :128] = kv[1, :, :, p * 128:(p + 1) * 128]
+
+    lane = lax.broadcasted_iota(jnp.int32, (share, 128), 1)
     own_rows = pl.ds(pl.multiple_of(m * share, share), share)
 
-    def attend(p):
-        cols = slice(p * 128, (p + 1) * 128)
-        pair_keys = keys[:, :, cols].reshape(2 * rows, 128)
-        pair_vals = jnp.concatenate(
-            [vals[:, :, cols].reshape(2 * rows, 128), jnp.ones((2 * rows, 128), b16)], axis=1)
-
-        for k in range(shards):
-            target = peers[k] if k < shards - 1 else m
-            here = pl.ds(pl.multiple_of(target * q_tile, q_tile), q_tile)
+    def attend(p, carry):
+        cols = pl.ds(pl.multiple_of(p * 128, 128), 128)
+
+        def step(k, carry):
+            here = pl.ds(pl.multiple_of(lax.rem(m + 1 + k, shards) * share, share), share)
             pair_q = queries[here, cols]
-            mask = bias[here, :]
             halves = []
             for h in range(2):
                 own = (lane < HD) if h == 0 else (lane >= HD)
                 head_q = jnp.where(own, pair_q, jnp.zeros_like(pair_q))
                 scores = lax.dot_general(
-                    head_q, pair_keys, (((1,), (1,)), ((), ())), preferred_element_type=f32) + mask
+                    head_q, kv[0, :, :, cols].reshape(2 * rows, 128),
+                    (((1,), (1,)), ((), ())), preferred_element_type=f32) + bias[here, :]
                 peak = jnp.max(scores, axis=-1, keepdims=True)
                 weights = jnp.exp(scores - peak).astype(b16)
-                mixed = jnp.dot(weights, pair_vals, preferred_element_type=f32)
+                mixed = jnp.dot(
+                    weights, vals_ones[p].reshape(2 * rows, 256), preferred_element_type=f32)
                 halves.append(mixed[:, :128] / mixed[:, 128:])
             mixed_rows = jnp.where(lane < HD, halves[0], halves[1]).astype(b16)
-            if k < shards - 1:
+
+            @pl.when(k < shards - 1)
+            def _():
                 att[p, k] = mixed_rows
                 a_copy(p, k).start()
-            else:
+
+            @pl.when(k == shards - 1)
+            def _():
                 att_in[m * pairs + p] = mixed_rows
 
-    attend(0)
-    landed(O, 0, 1)
-    go(O, 2, 4, 5)
-    for p in range(1, pairs):
-        attend(p)
+            return carry
+
+        lax.fori_loop(0, shards, step, 0)
+
+        @pl.when(p == 0)
+        def _():
+            landed(O, 0, 1)
+            go(O, 2, 4, 5)
+            landed(U, 0, 1)
+            go(U, 2, 4, 5)
+
+        return carry
+
+    lax.fori_loop(0, pairs, attend, 0)
     landed(O, 2)
     go(O, 6)
-    go(W, 1, 3)
-    landed(U, 0, 1)
-    go(U, 2, 4, 5)
+    landed(U, 2)
+    go(U, 6)
     landed(O, 3, 4, 5, 6)
     for p in range(pairs):
         for k in range(shards - 1):
@@ -419,18 +446,27 @@
 
     n_wide = 256
     o_parts = n_wide // part
-    joined = jnp.concatenate([att_in[i] for i in range(shards * pairs)], axis=1)
-
-    for n in range(width // n_wide):
-        block = full_o[n * o_parts:(n + 1) * o_parts].reshape(n_wide, width)
-        sums[:, n * n_wide:(n + 1) * n_wide] = lax.dot_general(
+
+    def out_step(n, carry):
+        here = pl.ds(pl.multiple_of(n * n_wide, n_wide), n_wide)
+        joined = jnp.concatenate([att_in[i] for i in range(shards * pairs)], axis=1)
+        block = full_o[pl.ds(n * o_parts, o_parts)].reshape(n_wide, width)
+        sums[:, here] = lax.dot_general(
             joined, block, (((1,), (1,)), ((), ())), preferred_element_type=f32)
-    normed[spot] = layer_norm(
-        hid[own_rows, :].astype(f32) + sums[...], gain1[...], shift1[...]).astype(b16)
+        return carry
+
+    lax.fori_loop(0, width // n_wide, out_step, 0)
+
+    def ln_step(i, carry):
+        here = pl.ds(pl.multiple_of(i * few, few), few)
+        there = pl.ds(pl.multiple_of(m * share + i * few, few), few)
+        normed[spot, here, :] = layer_norm(
+            hid[there, :].astype(f32) + sums[here, :], gain1[...], shift1[...]).astype(b16)
+        return carry
+
+    lax.fori_loop(0, share // few, ln_step, 0)
     for k in (1, 0, 2):
         n_copy(k).start()
-    landed(U, 2)
-    go(U, 6)
     landed(W, 0, 1)
     go(W, 2, 4, 5)
     landed(U, 3, 4, 5, 6)
@@ -442,59 +478,87 @@
                      + group_r // 2 % 2 * 2 + z_r % 2)
     d_parts = tile // part
 
-    def up(batch, spots):
-        tokens = jnp.concatenate([normed[i] for i in spots], axis=0)
+    def feed(batch, carry):
+        first = spot * (1 - batch) + square_spot[2] * batch
+        second = square_spot[1] * (1 - batch) + square_spot[0] * batch
+
+        @pl.when(batch == 0)
+        def _():
+            n_copy(1).wait_recv()
+
+        @pl.when(batch == 1)
+        def _():
+            n_copy(0).wait_recv()
+            n_copy(2).wait_recv()
 
         def up_step(n, carry):
             here = pl.ds(pl.multiple_of(n * n_wide, n_wide), n_wide)
             block = jnp.concatenate([full_u[r, :, here] for r in order], axis=0)
+            tokens = jnp.concatenate([normed[first], normed[second]], axis=0)
             pre = jnp.dot(tokens, block, preferred_element_type=f32)
-            act[batch, :, here] = (0.5 * pre * (1.0 + lax.erf(pre * (0.5 ** 0.5)))).astype(b16)
+            act[:, here] = (0.5 * pre * (1.0 + lax.erf(pre * (0.5 ** 0.5)))).astype(b16)
             return carry
 
         lax.fori_loop(0, lh // n_wide, up_step, 0)
 
-    def down(batch, n):
-        block = jnp.concatenate(
-            [full_d[r] for r in order[n * d_parts:(n + 1) * d_parts]], axis=0)
-        return lax.dot_general(
-            act[batch], block, (((1,), (1,)), ((), ())), preferred_element_type=f32)
-
-    n_copy(1).wait_recv()
-    up(0, (spot, square_spot[1]))
-    landed(W, 2)
-    go(W, 6)
-    landed(W, 3, 4, 5, 6)
-    for n in range(tiles):
-        term = down(0, n)
-        rs_send[1, n] = term[share:].astype(b16)
-        r_copy(n, 1).start()
-        sums[:, n * tile:(n + 1) * tile] = term[:share]
-    n_copy(0).wait_recv()
-    n_copy(2).wait_recv()
-    up(1, (square_spot[2], square_spot[0]))
-    for n in range(tiles):
-        term = down(1, n)
-        rs_send[2, n] = term[:share].astype(b16)
-        r_copy(n, 2).start()
-        rs_send[0, n] = term[share:].astype(b16)
-        r_copy(n, 0).start()
-    for n in range(tiles):
-        cols = slice(n * tile, (n + 1) * tile)
+        @pl.when(batch == 0)
+        def _():
+            landed(W, 2)
+            go(W, 6)
+            landed(W, 3, 4, 5, 6)
+
+        def down_step(n, carry):
+            start = n // 2 * 16 + lax.rem(n, 2) * 2
+            block = jnp.concatenate(
+                [full_d[start + i // 4 * 8 + i % 4 // 2 * 4 + i % 2] for i in range(d_parts)], axis=0)
+            term = lax.dot_general(
+                act[...], block, (((1,), (1,)), ((), ())), preferred_element_type=f32)
+
+            @pl.when(batch == 0)
+            def _():
+                rs_send[1, n] = term[share:].astype(b16)
+                r_copy(n, 1).start()
+                sums[:, pl.ds(pl.multiple_of(n * tile, tile), tile)] = term[:share]
+
+            @pl.when(batch == 1)
+            def _():
+                rs_send[2, n] = term[:share].astype(b16)
+                r_copy(n, 2).start()
+                rs_send[0, n] = term[share:].astype(b16)
+                r_copy(n, 0).start()
+
+            return carry
+
+        lax.fori_loop(0, tiles, down_step, 0)
+        return carry
+
+    lax.fori_loop(0, 2, feed, 0)
+
+    def total_step(n, carry):
+        cols = pl.ds(pl.multiple_of(n * tile, tile), tile)
         total = normed[spot, :, cols].astype(f32) + sums[:, cols]
         for k in (1, 0, 2):
             r_copy(n, k).wait_recv()
             total = total + rs_recv[k, n].astype(f32)
         sums[:, cols] = total
-    out[...] = layer_norm(sums[...], gain2[...], shift2[...]).astype(b16)
+        return carry
+
+    lax.fori_loop(0, tiles, total_step, 0)
+
+    def last_step(i, carry):
+        here = pl.ds(pl.multiple_of(i * few, few), few)
+        out[here, :] = layer_norm(sums[here, :], gain2[...], shift2[...]).astype(b16)
+        return carry
+
+    lax.fori_loop(0, share // few, last_step, 0)
 
     for kind in (Q, O, U, W):
         for k in range(shards - 1):
             z_copy(kind, k).wait_send()
         for step in range(7):
             p_copy(kind, step).wait_send()
-    kv_copy(keys, 0).wait_send()
-    kv_copy(vals, 1).wait_send()
+    for i in range(2):
+        kv_copy(i).wait_send()
     for k in range(shards - 1):
         n_copy(k).wait_send()
         for p in range(pairs):
@@ -547,13 +611,13 @@
             pltpu.VMEM((parts, part, lh), b16),
             pltpu.VMEM((rows, 2 * rows), f32),
             pltpu.VMEM((rows, lw), b16),
-            pltpu.VMEM((2, rows, lw), b16),
-            pltpu.VMEM((2, rows, lw), b16),
+            pltpu.VMEM((2, 2, rows, lw), b16),
+            pltpu.VMEM((pairs, 2, rows, 256), b16),
             pltpu.VMEM((pairs, others, share, 128), b16),
             pltpu.VMEM((shards * pairs, share, 128), b16),
             pltpu.VMEM((share, width), f32),
             pltpu.VMEM((shards, share, width), b16),
-            pltpu.VMEM((2, rows // 2, lh), b16),
+            pltpu.VMEM((rows // 2, lh), b16),
             pltpu.VMEM((others, tiles, share, tile), b16),
             pltpu.VMEM((others, tiles, share, tile), b16),
             dma((5,)),
@@ -565,7 +629,7 @@
             dma((tiles, others)), dma((tiles, others)),
         ],
         compiler_params=pltpu.CompilerParams(
-            collective_id=0, has_side_effects=True, vmem_limit_bytes=60 * 1024 * 1024),
+            collective_id=0, has_side_effects=True, vmem_limit_bytes=56 * 1024 * 1024),
         cost_estimate=pl.CostEstimate(
             flops=6 * rows * width * (4 * lw + 2 * lh), bytes_accessed=16 * 1024 * 1024,
             transcendentals=0),

time: 86.1 us -> 88.7 us (1.030); the launches traced: 85.8 us -> 87 us
  Pallas kernels: 80.2 us -> 81.4 us
    pallas_call x1, Pallas kernels: 80.2 us -> 81.4 us  [kernel_body(): pl.pallas_call(functools.partial(layer_kernel, shards), out_shape=(jax.Sh...]
where the time goes in v4:
time: 88.7 us; the launch traced here: 87 us
  Pallas kernels  81.4 us (92%)
  local copies, waits for them, and re-layouts  5 us (6%)
    pallas_call x1, Pallas kernels, kernel_body(): pl.pallas_call(functools.partial(layer_kernel, shards), out_shape=(jax.Sh...  81.4 us
    unnamed x9, local copies, waits for them, and re-layouts  4.14 us

profile of v4, /device:TPU:21, one launch (start us, length us, event | category | flops | bytes accessed | tf_op | source)
XLA Modules:
  0.0 87.0 jit_solution(1219137916470892801)
XLA Ops:
  0.6 0.0 copy-start.2
  0.6 0.7 copy-done.2
  1.3 0.9 copy.13.id_col
  2.2 81.4 %encoder_layer.1 = (bf16[128,1024]{1,0:T(8,128)(2,1)}, bf16[512,256]{1,0:T(8,128)(2,1)}, bf16[512,256]{1,0:T(8,128)(2,1)}) custom-call(bf16[512,1024]{1,0:T(8,128)(2,1)} %hid_in.1, s32[512,1]{1,0:T(8,128)} %copy.13.id_col, s32[1,512]{1,0:T(1,128)} %bitcast.6, f32[32,3072]{1,0:T(8,128)} %w_qkv_in.1, f32[32,1024]{1,0:T(8,128)} %w_out_in.1, ...), custom_call_target="tpu_custom_call" | custom-call | flops 9663676416 | bytes 16777216 | tf_op jit(solution)/shard_map/encoder_layer/pallas_call | solution.py:589
  83.6 0.0 copy-start.1
  83.6 1.7 %copy.17 = bf16[128,1024]{1,0:T(8,128)(2,1)} copy(bf16[128,1024]{1,0:T(8,128)(2,1)} %get-tuple-element.6) | data formatting | bytes 524288
  85.3 0.0 copy-done.1
  85.3 0.0 copy-start
  85.3 0.7 copy.18
  86.0 0.3 copy-done
  86.3 0.7 copy.19
Async XLA Ops:
  0.6 0.7 copy-start.2
  83.6 1.7 %copy-start.1 = (bf16[512,256]{1,0:T(8,128)(2,1)S(1)}, bf16[512,256]{1,0:T(8,128)(2,1)}, u32[]{:S(2)}) copy-start(bf16[512,256]{1,0:T(8,128)(2,1)} %get-tuple-element.7) | copy-start | bytes 786436
  85.3 1.0 %copy-start = (bf16[512,256]{1,0:T(8,128)(2,1)S(1)}, bf16[512,256]{1,0:T(8,128)(2,1)}, u32[]{:S(2)}) copy-start(bf16[512,256]{1,0:T(8,128)(2,1)} %get-tuple-element.8) | copy-start | bytes 786436

commit v5 on v4

--- a/solution.py
+++ b/solution.py
@@ -349,14 +349,14 @@
     arrived(Q)
     go(Q, 0, 1, 3)
     depart(O)
-    arrived(U)
-    go(U, 0)
-    depart(W)
     loads[4].wait()
     landed(Q, 0, 1)
     go(Q, 2, 4, 5)
     arrived(O)
     go(O, 0, 1, 3)
+    arrived(U)
+    go(U, 0)
+    depart(W)
     landed(Q, 2)
     go(Q, 6)
     landed(Q, 3, 4, 5, 6)
@@ -380,12 +380,12 @@
 
     lax.fori_loop(0, 3, project, 0)
     go(U, 1, 3)
-    arrived(W)
-    go(W, 0, 1, 3)
     k_out[...] = kv[0, 0]
     v_out[...] = kv[1, 0]
     for i in range(2):
         kv_copy(i).wait_recv()
+    landed(O, 0, 1)
+    go(O, 2, 4, 5)
     for p in range(pairs):
         vals_ones[p, :, :, :128] = kv[1, :, :, p * 128:(p + 1) * 128]
 
@@ -427,18 +427,19 @@
 
         @pl.when(p == 0)
         def _():
-            landed(O, 0, 1)
-            go(O, 2, 4, 5)
-            landed(U, 0, 1)
-            go(U, 2, 4, 5)
+            landed(O, 2)
+            go(O, 6)
+            arrived(W)
+            landed(U, 0)
+            go(U, 2, 4)
+            go(W, 0)
 
         return carry
 
     lax.fori_loop(0, pairs, attend, 0)
-    landed(O, 2)
-    go(O, 6)
-    landed(U, 2)
-    go(U, 6)
+    landed(U, 1)
+    go(U, 5)
+    go(W, 1, 3)
     landed(O, 3, 4, 5, 6)
     for p in range(pairs):
         for k in range(shards - 1):
@@ -467,8 +468,12 @@
     lax.fori_loop(0, share // few, ln_step, 0)
     for k in (1, 0, 2):
         n_copy(k).start()
-    landed(W, 0, 1)
-    go(W, 2, 4, 5)
+    landed(U, 2)
+    go(U, 6)
+    landed(W, 0)
+    go(W, 2, 4)
+    landed(W, 1)
+    go(W, 5)
     landed(U, 3, 4, 5, 6)
 
     order = []

time: 88.7 us -> 91.9 us (1.036); the launches traced: 87 us -> 91.7 us
  Pallas kernels: 81.4 us -> 86 us
    pallas_call x1, Pallas kernels: 81.4 us -> 86 us  [kernel_body(): pl.pallas_call(functools.partial(layer_kernel, shards), out_shape=(jax.Sh...]
where the time goes in v5:
time: 91.9 us; the launch traced here: 91.7 us
  Pallas kernels  86 us (94%)
  local copies, waits for them, and re-layouts  5 us (5%)
    pallas_call x1, Pallas kernels, kernel_body(): pl.pallas_call(functools.partial(layer_kernel, shards), out_shape=(jax.Sh...  86 us
    unnamed x9, local copies, waits for them, and re-layouts  4.14 us

profile of v5, /device:TPU:21, one launch (start us, length us, event | category | flops | bytes accessed | tf_op | source)
XLA Modules:
  0.0 91.7 jit_solution(10467760620871283398)
XLA Ops:
  0.6 0.0 copy-start.2
  0.6 0.7 copy-done.2
  1.3 0.9 copy.13.id_col
  2.2 86.0 %encoder_layer.1 = (bf16[128,1024]{1,0:T(8,128)(2,1)}, bf16[512,256]{1,0:T(8,128)(2,1)}, bf16[512,256]{1,0:T(8,128)(2,1)}) custom-call(bf16[512,1024]{1,0:T(8,128)(2,1)} %hid_in.1, s32[512,1]{1,0:T(8,128)} %copy.13.id_col, s32[1,512]{1,0:T(1,128)} %bitcast.6, f32[32,3072]{1,0:T(8,128)} %w_qkv_in.1, f32[32,1024]{1,0:T(8,128)} %w_out_in.1, ...), custom_call_target="tpu_custom_call" | custom-call | flops 9663676416 | bytes 16777216 | tf_op jit(solution)/shard_map/encoder_layer/pallas_call | solution.py:594
  88.2 0.0 copy-start.1
  88.2 1.7 %copy.17 = bf16[128,1024]{1,0:T(8,128)(2,1)} copy(bf16[128,1024]{1,0:T(8,128)(2,1)} %get-tuple-element.6) | data formatting | bytes 524288
  90.0 0.0 copy-done.1
  90.0 0.0 copy-start
  90.0 0.7 copy.18
  90.7 0.3 copy-done
  91.0 0.7 copy.19
Async XLA Ops:
  0.6 0.7 copy-start.2
  88.2 1.7 %copy-start.1 = (bf16[512,256]{1,0:T(8,128)(2,1)S(1)}, bf16[512,256]{1,0:T(8,128)(2,1)}, u32[]{:S(2)}) copy-start(bf16[512,256]{1,0:T(8,128)(2,1)} %get-tuple-element.7) | copy-start | bytes 786436
  90.0 1.0 %copy-start = (bf16[512,256]{1,0:T(8,128)(2,1)S(1)}, bf16[512,256]{1,0:T(8,128)(2,1)}, u32[]{:S(2)}) copy-start(bf16[512,256]{1,0:T(8,128)(2,1)} %get-tuple-element.8) | copy-start | bytes 786436

commit v6 on v4

--- a/solution.py
+++ b/solution.py
@@ -324,10 +324,9 @@
             z_copy(kind, k).start()
 
     depart(Q)
-    stage(U)
-    depart(U)
-    stage(O)
-    stage(W)
+    for kind in (U, O, W):
+        stage(kind)
+        depart(kind)
 
     long_id = jnp.where(core == 0, id_col[rows - 1:rows, :], id_col[0:1, :])
     slot = sib * rows + lax.broadcasted_iota(jnp.int32, (1, rows), 1)
@@ -348,15 +347,15 @@
 
     arrived(Q)
     go(Q, 0, 1, 3)
-    depart(O)
     arrived(U)
-    go(U, 0)
-    depart(W)
+    go(U, 0, 1, 3)
     loads[4].wait()
     landed(Q, 0, 1)
     go(Q, 2, 4, 5)
     arrived(O)
     go(O, 0, 1, 3)
+    arrived(W)
+    go(W, 0, 1, 3)
     landed(Q, 2)
     go(Q, 6)
     landed(Q, 3, 4, 5, 6)
@@ -379,9 +378,6 @@
         return carry
 
     lax.fori_loop(0, 3, project, 0)
-    go(U, 1, 3)
-    arrived(W)
-    go(W, 0, 1, 3)
     k_out[...] = kv[0, 0]
     v_out[...] = kv[1, 0]
     for i in range(2):
@@ -389,56 +385,60 @@
     for p in range(pairs):
         vals_ones[p, :, :, :128] = kv[1, :, :, p * 128:(p + 1) * 128]
 
-    lane = lax.broadcasted_iota(jnp.int32, (share, 128), 1)
+    lane = lax.broadcasted_iota(jnp.int32, (2 * share, 128), 1)
     own_rows = pl.ds(pl.multiple_of(m * share, share), share)
 
     def attend(p, carry):
         cols = pl.ds(pl.multiple_of(p * 128, 128), 128)
 
-        def step(k, carry):
-            here = pl.ds(pl.multiple_of(lax.rem(m + 1 + k, shards) * share, share), share)
-            pair_q = queries[here, cols]
+        def step(j, carry):
+            spans = [
+                pl.ds(pl.multiple_of(lax.rem(m + 1 + 2 * j + i, shards) * share, share), share)
+                for i in range(2)
+            ]
+            pair_q = jnp.concatenate([queries[here, cols] for here in spans], axis=0)
             halves = []
             for h in range(2):
                 own = (lane < HD) if h == 0 else (lane >= HD)
                 head_q = jnp.where(own, pair_q, jnp.zeros_like(pair_q))
                 scores = lax.dot_general(
                     head_q, kv[0, :, :, cols].reshape(2 * rows, 128),
-                    (((1,), (1,)), ((), ())), preferred_element_type=f32) + bias[here, :]
+                    (((1,), (1,)), ((), ())), preferred_element_type=f32)
+                scores = scores + jnp.concatenate([bias[here, :] for here in spans], axis=0)
                 peak = jnp.max(scores, axis=-1, keepdims=True)
                 weights = jnp.exp(scores - peak).astype(b16)
                 mixed = jnp.dot(
                     weights, vals_ones[p].reshape(2 * rows, 256), preferred_element_type=f32)
                 halves.append(mixed[:, :128] / mixed[:, 128:])
             mixed_rows = jnp.where(lane < HD, halves[0], halves[1]).astype(b16)
-
-            @pl.when(k < shards - 1)
-            def _():
-                att[p, k] = mixed_rows
-                a_copy(p, k).start()
-
-            @pl.when(k == shards - 1)
-            def _():
-                att_in[m * pairs + p] = mixed_rows
+            for i in range(2):
+                k = 2 * j + i
+
+                @pl.when(k < shards - 1)
+                def _():
+                    att[p, k] = mixed_rows[i * share:(i + 1) * share]
+                    a_copy(p, k).start()
+
+                @pl.when(k == shards - 1)
+                def _():
+                    att_in[m * pairs + p] = mixed_rows[i * share:(i + 1) * share]
 
             return carry
 
-        lax.fori_loop(0, shards, step, 0)
+        lax.fori_loop(0, shards // 2, step, 0)
 
         @pl.when(p == 0)
         def _():
             landed(O, 0, 1)
             go(O, 2, 4, 5)
-            landed(U, 0, 1)
-            go(U, 2, 4, 5)
 
         return carry
 
     lax.fori_loop(0, pairs, attend, 0)
     landed(O, 2)
     go(O, 6)
-    landed(U, 2)
-    go(U, 6)
+    landed(U, 0, 1)
+    go(U, 2, 4, 5)
     landed(O, 3, 4, 5, 6)
     for p in range(pairs):
         for k in range(shards - 1):
@@ -467,6 +467,8 @@
     lax.fori_loop(0, share // few, ln_step, 0)
     for k in (1, 0, 2):
         n_copy(k).start()
+    landed(U, 2)
+    go(U, 6)
     landed(W, 0, 1)
     go(W, 2, 4, 5)
     landed(U, 3, 4, 5, 6)

time: 88.7 us -> 84.2 us (0.949); the launches traced: 87 us -> 84 us
  Pallas kernels: 81.4 us -> 78.3 us
    pallas_call x1, Pallas kernels: 81.4 us -> 78.3 us  [kernel_body(): pl.pallas_call(functools.partial(layer_kernel, shards), out_shape=(jax.Sh...]
where the time goes in v6:
time: 84.2 us; the launch traced here: 84 us
  Pallas kernels  78.3 us (93%)
  local copies, waits for them, and re-layouts  5 us (6%)
    pallas_call x1, Pallas kernels, kernel_body(): pl.pallas_call(functools.partial(layer_kernel, shards), out_shape=(jax.Sh...  78.3 us
    unnamed x9, local copies, waits for them, and re-layouts  4.14 us

profile of v6, /device:TPU:21, one launch (start us, length us, event | category | flops | bytes accessed | tf_op | source)
XLA Modules:
  0.0 84.0 jit_solution(10215522223484875481)
XLA Ops:
  0.6 0.0 copy-start.2
  0.6 0.7 copy-done.2
  1.3 0.9 %copy.13.id_col = s32[512,1]{1,0:T(8,128)} copy(s32[512,1]{0,1:T(1,128)S(1)} %bitcast.7) | data formatting | bytes 4096 | tf_op jit(solution)/shard_map/reshape | solution.py:640
  2.2 78.3 %encoder_layer.1 = (bf16[128,1024]{1,0:T(8,128)(2,1)}, bf16[512,256]{1,0:T(8,128)(2,1)}, bf16[512,256]{1,0:T(8,128)(2,1)}) custom-call(bf16[512,1024]{1,0:T(8,128)(2,1)} %hid_in.1, s32[512,1]{1,0:T(8,128)} %copy.13.id_col, s32[1,512]{1,0:T(1,128)} %bitcast.6, f32[32,3072]{1,0:T(8,128)} %w_qkv_in.1, f32[32,1024]{1,0:T(8,128)} %w_out_in.1, ...), custom_call_target="tpu_custom_call" | custom-call | flops 9663676416 | bytes 16777216 | tf_op jit(solution)/shard_map/encoder_layer/pallas_call | solution.py:591
  80.5 0.0 copy-start.1
  80.5 1.7 %copy.17 = bf16[128,1024]{1,0:T(8,128)(2,1)} copy(bf16[128,1024]{1,0:T(8,128)(2,1)} %get-tuple-element.6) | data formatting | bytes 524288
  82.2 0.0 copy-done.1
  82.2 0.0 copy-start
  82.2 0.7 copy.18
  82.9 0.3 copy-done
  83.3 0.7 copy.19
Async XLA Ops:
  0.6 0.7 copy-start.2
  80.5 1.7 %copy-start.1 = (bf16[512,256]{1,0:T(8,128)(2,1)S(1)}, bf16[512,256]{1,0:T(8,128)(2,1)}, u32[]{:S(2)}) copy-start(bf16[512,256]{1,0:T(8,128)(2,1)} %get-tuple-element.7) | copy-start | bytes 786436
  82.2 1.0 %copy-start = (bf16[512,256]{1,0:T(8,128)(2,1)S(1)}, bf16[512,256]{1,0:T(8,128)(2,1)}, u32[]{:S(2)}) copy-start(bf16[512,256]{1,0:T(8,128)(2,1)} %get-tuple-element.8) | copy-start | bytes 786436

commit v7 on v6

--- a/solution.py
+++ b/solution.py
@@ -355,7 +355,7 @@
     arrived(O)
     go(O, 0, 1, 3)
     arrived(W)
-    go(W, 0, 1, 3)
+    go(W, 1, 3)
     landed(Q, 2)
     go(Q, 6)
     landed(Q, 3, 4, 5, 6)
@@ -378,6 +378,7 @@
         return carry
 
     lax.fori_loop(0, 3, project, 0)
+    go(W, 0)
     k_out[...] = kv[0, 0]
     v_out[...] = kv[1, 0]
     for i in range(2):
@@ -386,7 +387,6 @@
         vals_ones[p, :, :, :128] = kv[1, :, :, p * 128:(p + 1) * 128]
 
     lane = lax.broadcasted_iota(jnp.int32, (2 * share, 128), 1)
-    own_rows = pl.ds(pl.multiple_of(m * share, share), share)
 
     def attend(p, carry):
         cols = pl.ds(pl.multiple_of(p * 128, 128), 128)
@@ -437,8 +437,6 @@
     lax.fori_loop(0, pairs, attend, 0)
     landed(O, 2)
     go(O, 6)
-    landed(U, 0, 1)
-    go(U, 2, 4, 5)
     landed(O, 3, 4, 5, 6)
     for p in range(pairs):
         for k in range(shards - 1):
@@ -467,10 +465,14 @@
     lax.fori_loop(0, share // few, ln_step, 0)
     for k in (1, 0, 2):
         n_copy(k).start()
+    landed(U, 0, 1)
+    go(U, 2, 4, 5)
+    landed(W, 1)
+    go(W, 5)
     landed(U, 2)
     go(U, 6)
-    landed(W, 0, 1)
-    go(W, 2, 4, 5)
+    landed(W, 0)
+    go(W, 2, 4)
     landed(U, 3, 4, 5, 6)
 
     order = []

time: 84.2 us -> 89.2 us (1.059); the launches traced: 84 us -> 87.5 us
  Pallas kernels: 78.3 us -> 81.8 us
    pallas_call x1, Pallas kernels: 78.3 us -> 81.8 us  [kernel_body(): pl.pallas_call(functools.partial(layer_kernel, shards), out_shape=(jax.Sh...]
where the time goes in v7:
time: 89.2 us; the launch traced here: 87.5 us
  Pallas kernels  81.8 us (92%)
  local copies, waits for them, and re-layouts  5 us (6%)
    pallas_call x1, Pallas kernels, kernel_body(): pl.pallas_call(functools.partial(layer_kernel, shards), out_shape=(jax.Sh...  81.8 us
    unnamed x9, local copies, waits for them, and re-layouts  4.14 us

profile of v7, /device:TPU:21, one launch (start us, length us, event | category | flops | bytes accessed | tf_op | source)
XLA Modules:
  0.0 87.5 jit_solution(10496788611190444022)
XLA Ops:
  0.6 0.0 copy-start.2
  0.6 0.7 copy-done.2
  1.3 0.9 copy.13.id_col
  2.2 81.8 %encoder_layer.1 = (bf16[128,1024]{1,0:T(8,128)(2,1)}, bf16[512,256]{1,0:T(8,128)(2,1)}, bf16[512,256]{1,0:T(8,128)(2,1)}) custom-call(bf16[512,1024]{1,0:T(8,128)(2,1)} %hid_in.1, s32[512,1]{1,0:T(8,128)} %copy.13.id_col, s32[1,512]{1,0:T(1,128)} %bitcast.6, f32[32,3072]{1,0:T(8,128)} %w_qkv_in.1, f32[32,1024]{1,0:T(8,128)} %w_out_in.1, ...), custom_call_target="tpu_custom_call" | custom-call | flops 9663676416 | bytes 16777216 | tf_op jit(solution)/shard_map/encoder_layer/pallas_call | solution.py:593
  84.0 0.0 copy-start.1
  84.0 1.7 %copy.17 = bf16[128,1024]{1,0:T(8,128)(2,1)} copy(bf16[128,1024]{1,0:T(8,128)(2,1)} %get-tuple-element.6) | data formatting | bytes 524288
  85.7 0.0 copy-done.1
  85.7 0.0 copy-start
  85.7 0.7 copy.18
  86.5 0.3 copy-done
  86.8 0.7 copy.19
Async XLA Ops:
  0.6 0.7 copy-start.2
  84.0 1.7 %copy-start.1 = (bf16[512,256]{1,0:T(8,128)(2,1)S(1)}, bf16[512,256]{1,0:T(8,128)(2,1)}, u32[]{:S(2)}) copy-start(bf16[512,256]{1,0:T(8,128)(2,1)} %get-tuple-element.7) | copy-start | bytes 786436
  85.7 1.0 %copy-start = (bf16[512,256]{1,0:T(8,128)(2,1)S(1)}, bf16[512,256]{1,0:T(8,128)(2,1)}, u32[]{:S(2)}) copy-start(bf16[512,256]{1,0:T(8,128)(2,1)} %get-tuple-element.8) | copy-start | bytes 786436

commit v8 on v6

--- a/solution.py
+++ b/solution.py
@@ -324,7 +324,7 @@
             z_copy(kind, k).start()
 
     depart(Q)
-    for kind in (U, O, W):
+    for kind in (U, W, O):
         stage(kind)
         depart(kind)
 
@@ -349,13 +349,13 @@
     go(Q, 0, 1, 3)
     arrived(U)
     go(U, 0, 1, 3)
+    arrived(W)
+    go(W, 0, 1, 3)
     loads[4].wait()
     landed(Q, 0, 1)
     go(Q, 2, 4, 5)
     arrived(O)
     go(O, 0, 1, 3)
-    arrived(W)
-    go(W, 0, 1, 3)
     landed(Q, 2)
     go(Q, 6)
     landed(Q, 3, 4, 5, 6)
@@ -439,6 +439,8 @@
     go(O, 6)
     landed(U, 0, 1)
     go(U, 2, 4, 5)
+    landed(W, 0, 1)
+    go(W, 2, 4, 5)
     landed(O, 3, 4, 5, 6)
     for p in range(pairs):
         for k in range(shards - 1):
@@ -469,8 +471,6 @@
         n_copy(k).start()
     landed(U, 2)
     go(U, 6)
-    landed(W, 0, 1)
-    go(W, 2, 4, 5)
     landed(U, 3, 4, 5, 6)
 
     order = []

time: 84.2 us -> 85.3 us (1.013)
  Pallas kernels: 78.3 us -> 79.4 us
    pallas_call x1, Pallas kernels: 78.3 us -> 79.4 us  [kernel_body(): pl.pallas_call(functools.partial(layer_kernel, shards), out_shape=(jax.Sh...]
where the time goes in v8:
time: 85.3 us; the launch traced here: 85.1 us
  Pallas kernels  79.4 us (93%)
  local copies, waits for them, and re-layouts  5 us (6%)
    pallas_call x1, Pallas kernels, kernel_body(): pl.pallas_call(functools.partial(layer_kernel, shards), out_shape=(jax.Sh...  79.4 us
    unnamed x9, local copies, waits for them, and re-layouts  4.14 us

profile of v8, /device:TPU:21, one launch (start us, length us, event | category | flops | bytes accessed | tf_op | source)
XLA Modules:
  0.0 85.1 jit_solution(1477044615869785264)
XLA Ops:
  0.6 0.0 copy-start.2
  0.6 0.7 copy-done.2
  1.3 0.9 %copy.13.id_col = s32[512,1]{1,0:T(8,128)} copy(s32[512,1]{0,1:T(1,128)S(1)} %bitcast.7) | data formatting | bytes 4096 | tf_op jit(solution)/shard_map/reshape | solution.py:640
  2.2 79.4 %encoder_layer.1 = (bf16[128,1024]{1,0:T(8,128)(2,1)}, bf16[512,256]{1,0:T(8,128)(2,1)}, bf16[512,256]{1,0:T(8,128)(2,1)}) custom-call(bf16[512,1024]{1,0:T(8,128)(2,1)} %hid_in.1, s32[512,1]{1,0:T(8,128)} %copy.13.id_col, s32[1,512]{1,0:T(1,128)} %bitcast.6, f32[32,3072]{1,0:T(8,128)} %w_qkv_in.1, f32[32,1024]{1,0:T(8,128)} %w_out_in.1, ...), custom_call_target="tpu_custom_call" | custom-call | flops 9663676416 | bytes 16777216 | tf_op jit(solution)/shard_map/encoder_layer/pallas_call | solution.py:591
  81.6 0.0 copy-start.1
  81.6 1.7 %copy.17 = bf16[128,1024]{1,0:T(8,128)(2,1)} copy(bf16[128,1024]{1,0:T(8,128)(2,1)} %get-tuple-element.6) | data formatting | bytes 524288
  83.3 0.0 copy-done.1
  83.3 0.0 copy-start
  83.3 0.7 copy.18
  84.0 0.3 copy-done
  84.4 0.7 copy.19
Async XLA Ops:
  0.6 0.7 copy-start.2
  81.6 1.7 %copy-start.1 = (bf16[512,256]{1,0:T(8,128)(2,1)S(1)}, bf16[512,256]{1,0:T(8,128)(2,1)}, u32[]{:S(2)}) copy-start(bf16[512,256]{1,0:T(8,128)(2,1)} %get-tuple-element.7) | copy-start | bytes 786436
  83.3 1.0 %copy-start = (bf16[512,256]{1,0:T(8,128)(2,1)S(1)}, bf16[512,256]{1,0:T(8,128)(2,1)}, u32[]{:S(2)}) copy-start(bf16[512,256]{1,0:T(8,128)(2,1)} %get-tuple-element.8) | copy-start | bytes 786436
